TPU v7x, 512 devices: a whole 4x8x8 slice. The times are simulated.
512 devices in a mesh: leaf: 8 (over x, core), sub: 64 (over z, y).
Axes of the slice: x: 4, y: 8, z: 8, core: 2. Of those that a mesh axis runs over, the one named last changes fastest.
Arguments:
- points: bfloat16 [131072, 64], P(('leaf', 'sub')), may hold values from -6 to 6
- omega: bfloat16 [131072, 256], P(('leaf', 'sub')), may hold values from -6 to 6
- samples: float32 [131072, 256], P(('leaf', 'sub')), may hold values from -48 to 48
- ranks: int32 [8, 4], P('leaf'), may hold values from 128 to 256, as said below
- leaf_skeleton: int32 [8, 256], P('leaf'), may hold values from 0 to 16383, as said below
- merge_skeleton: int32 [8, 3, 256], P('leaf'), may hold values from 0 to 511, as said below
Outputs:
- leaf_interp: float32 [131072, 256], P(('leaf', 'sub'))
- node_interp: float32 [8, 3, 512, 256], P('leaf')
- couplings: float32 [8, 3, 256, 256], P('leaf')
- top_compressed: float32 [8, 256, 256], P('leaf')
Inputs may be any that keep to these rules, and one draw needn't show every extreme that they name: ranks[i, l] is the rank of the level-l node holding leaf i (leaves with equal i >> l share it); 256 is reached. `leaf_skeleton`: row i lists 256 distinct point indices within leaf i; the first ranks[i, 0] are its skeleton. merge_skeleton[i, l - 1] lists 256 distinct candidate rows of the level-l node holding leaf i, equal for all its leaves; candidate j < 256 is the lower child's row j, else the upper child's row j - 256; the first ranks[i, l] name rows below the owning child's rank.
All inputs are finite; a program needn't handle non-finite values.
Results may differ from a plain program's by a relative error of at most 0.00076.
Values may be sent and summed in bfloat16 or wider, within the bound.
A program may use at most 128 MiB of HBM per device.

v0:
```python
import jax
import jax.numpy as jnp
from jax import lax
from jax.sharding import PartitionSpec as P

LEVELS = 3


def partner(value, axis, stride):
    mask = 2**stride
    pairs = [(source, source ^ mask) for source in range(lax.axis_size(axis))]
    return lax.ppermute(value, axis, pairs)


def kernel(left, right):
    cross = jnp.einsum("id,jd->ij", left, right, preferred_element_type=jnp.float32)
    left_sq = jnp.sum(jnp.square(left.astype(jnp.float32)), axis=1)
    right_sq = jnp.sum(jnp.square(right.astype(jnp.float32)), axis=1)
    return jnp.exp(-(left_sq[:, None] + right_sq[None, :] - 2.0 * cross) / (0.5 * left.shape[1]))


def factorize(picked):
    gram = jnp.dot(
        picked, picked.T, precision=lax.Precision.HIGHEST, preferred_element_type=jnp.float32
    )
    shift = jnp.sum(picked * picked) / picked.shape[0] + 1e-06
    return jnp.linalg.cholesky(gram + shift * jnp.eye(picked.shape[0], dtype=jnp.float32))


def interpolate(factor, candid, picked):
    right_side = jnp.einsum("rs,ns->rn", picked, candid, precision=lax.Precision.HIGHEST)
    return jax.scipy.linalg.cho_solve((factor, True), right_side).T


def shards(points, omega, samples, ranks, leaf_skeleton, merge_skeleton):
    rows = points.shape[0]
    width = leaf_skeleton.shape[1]
    sub_pos = lax.axis_index("sub")
    leaf_pos = lax.axis_index("leaf")
    weights = kernel(points, lax.all_gather(points, "sub", axis=0, tiled=True)).astype(jnp.bfloat16)
    diag = jnp.dot(
        weights,
        lax.all_gather(omega, "sub", axis=0, tiled=True),
        preferred_element_type=jnp.float32,
    )
    resid = samples - diag
    live = (jnp.arange(width) < ranks[0, 0]).astype(jnp.float32)
    offsets = leaf_skeleton[0] - sub_pos * rows
    owned = ((offsets >= 0) & (offsets < rows)).astype(jnp.float32) * live
    places = jnp.clip(offsets, 0, rows - 1)
    part_rows = jnp.take(resid, places, axis=0) * owned[:, None]
    part_points = jnp.take(points, places, axis=0).astype(jnp.float32) * owned[:, None]
    omega_wide = omega.astype(jnp.float32)
    picked, chosen = lax.psum((part_rows, part_points), "sub")
    factor = factorize(picked)
    leaf_interp = interpolate(factor, resid, picked)
    local_part = jnp.einsum("nr,ns->rs", leaf_interp, omega_wide, precision=lax.Precision.HIGHEST)
    compressed = lax.psum(local_part, "sub")
    interp_levels = []
    couple_levels = []
    for height in range(1, LEVELS + 1):
        other_points, other_rows, other_comp, other_live = partner(
            (chosen, picked, compressed, live), "leaf", height - 1
        )
        coupling = (
            live[:, None]
            * other_live[None, :]
            * kernel(chosen.astype(jnp.bfloat16), other_points.astype(jnp.bfloat16))
        )
        own_new = picked - jnp.dot(coupling, other_comp, precision=lax.Precision.HIGHEST)
        other_new = other_rows - jnp.einsum(
            "ij,is->js", coupling, compressed, precision=lax.Precision.HIGHEST
        )
        is_lower = leaf_pos // 2 ** (height - 1) % 2 == 0
        cand_y = jnp.where(
            is_lower,
            jnp.concatenate([own_new, other_new], axis=0),
            jnp.concatenate([other_new, own_new], axis=0),
        )
        cand_x = jnp.where(
            is_lower,
            jnp.concatenate([chosen, other_points], axis=0),
            jnp.concatenate([other_points, chosen], axis=0),
        )
        cand_o = jnp.where(
            is_lower,
            jnp.concatenate([compressed, other_comp], axis=0),
            jnp.concatenate([other_comp, compressed], axis=0),
        )
        live = (jnp.arange(width) < ranks[0, height]).astype(jnp.float32)
        indices = merge_skeleton[0, height - 1]
        picked = jnp.take(cand_y, indices, axis=0) * live[:, None]
        chosen = jnp.take(cand_x, indices, axis=0) * live[:, None]
        factor = factorize(picked)
        node_matrix = interpolate(factor, cand_y, picked)
        compressed = jnp.einsum("nr,ns->rs", node_matrix, cand_o, precision=lax.Precision.HIGHEST)
        interp_levels.append(node_matrix)
        couple_levels.append(coupling)
    node_interp = jnp.stack(interp_levels, axis=0)[None]
    couplings = jnp.stack(couple_levels, axis=0)[None]
    return (leaf_interp, node_interp, couplings, compressed[None])


def solution(mesh):
    in_specs = (
        P(("leaf", "sub"), None),
        P(("leaf", "sub"), None),
        P(("leaf", "sub"), None),
        P("leaf", None),
        P("leaf", None),
        P("leaf", None, None),
    )
    out_specs = (
        P(("leaf", "sub"), None),
        P("leaf", None, None, None),
        P("leaf", None, None, None),
        P("leaf", None, None),
    )
    return jax.shard_map(shards, mesh=mesh, in_specs=in_specs, out_specs=out_specs, check_vma=False)
```

profile of v0, /device:TPU:1, one launch (start us, length us, event | category | flops | bytes accessed | tf_op | source)
XLA Modules:
  0.0 842.3 jit_solution(15058260484745908838)
XLA Ops:
  10.8 8.8 %collective-permute-start = (f32[256]{0:T(256)S(1)}, f32[256]{0:T(256)S(1)}, u32[]{:S(2)}, u32[]{:S(2)}) collective-permute-start(f32[256]{0:T(256)S(1)} %fusion.116), channel_id=1, source_target_pairs={{0,64},{64,0},{128,192},{192,128},{256,320},{320,256},{384,448},{4... | collective-permute-start | bytes 3080 | tf_op jit(solution)/shard_map/ppermute | solution.py:12
  20.2 1.9 collective-permute-start.4
  22.8 1.9 collective-permute-start.8
  29.0 67.4 %all-gather.3.cloned.1.call-done = bf16[16384,64]{0,1:T(8,128)(2,1)} async-done(((bf16[256,64]{0,1:T(8,128)(2,1)}), bf16[16384,64]{0,1:T(8,128)(2,1)}) %all-gather.3.cloned.1.call-update) | async-done | bytes 2097168 | tf_op jit(solution)/shard_map/all_gather | solution.py:40
  96.4 2.1 multiply_reduce_fusion
  98.5 99.6 %all-gather.5.cloned.1.call-done = bf16[16384,256]{1,0:T(8,128)(2,1)} async-done(((bf16[256,256]{1,0:T(8,128)(2,1)}), bf16[16384,256]{1,0:T(8,128)(2,1)}) %all-gather.5.cloned.1.call-update) | async-done | bytes 8388624 | tf_op jit(solution)/shard_map/all_gather | solution.py:43
  198.1 8.7 %fusion.6 = f32[256,256]{1,0:T(8,128)S(1)} fusion(f32[256,256]{1,0:T(8,128)} %param.15, bf16[16384,256]{1,0:T(8,128)(2,1)} %all-gather.5.cloned.1.call-done, bf16[256,64]{0,1:T(8,128)(2,1)} %param.13, bf16[16384,64]{0,1:T(8,128)(2,1)} %all-gather.3.cloned.1.call-done, f32[16384]{0:T(1024)S(1)} %multiply_reduce_fusion, f32[256]{0:T(256)S(1)} %multiply_reduce_fusion.11), kind=kOutput, calls=%fused_computation.24 | convolution fusion | flops 2709585920 | bytes 11109376 | tf_op jit(solution)/shard_map/dot_general | solution.py:41
  210.8 144.1 %all-reduce.5.cloned.1.call-done = f32[256,256]{1,0:T(8,128)} async-done(((f32[256,256]{1,0:T(8,128)}), f32[256,256]{1,0:T(8,128)}) %all-reduce.5.cloned.1.call-update) | async-done | bytes 262160 | tf_op jit(solution)/shard_map/psum | solution.py:54
  355.0 1.7 multiply_reduce_fusion.4
  358.9 11.7 %cholesky.214 = f32[128,128]{1,0:T(8,128)S(1)} custom-call(f32[128,128]{1,0:T(8,128)S(1)} %cholesky.346), custom_call_target="Cholesky" | custom-call | tf_op jit(solution)/shard_map/jit(cholesky)/cholesky | solution.py:27
  370.8 9.8 %custom-call.26 = f32[1,128,128]{1,2,0:T(8,128)S(1)} custom-call(f32[1,128,128]{2,1,0:T(8,128)S(1)} %get-tuple-element.120), custom_call_target="InvertDiagBlocksLowerTriangular" | custom-call | tf_op jit(solution)/shard_map/jit(cholesky)/cholesky | solution.py:27
  381.2 11.7 %cholesky.231 = f32[128,128]{1,0:T(8,128)S(1)} custom-call(f32[128,128]{1,0:T(8,128)S(1)} %convolution_subtract_fusion.17), custom_call_target="Cholesky" | custom-call | tf_op jit(solution)/shard_map/jit(cholesky)/cholesky | solution.py:27
  395.3 4.6 while.7
  399.9 19.7 %custom-call.20 = f32[2,128,128]{1,2,0:T(8,128)S(1)} custom-call(f32[2,128,128]{2,1,0:T(8,128)S(1)} %get-tuple-element.23), custom_call_target="InvertDiagBlocksLowerTriangular" | custom-call | tf_op jit(solution)/shard_map/jit(_cho_solve)/triangular_solve | solution.py:32
  424.5 6.6 collective-permute-start.3
  431.2 143.8 %all-reduce.7.cloned.1.call-done = (f32[256,256]{1,0:T(8,128)}, f32[256,64]{1,0:T(8,128)}) async-done(((f32[256,256]{1,0:T(8,128)}, f32[256,64]{1,0:T(8,128)}), (f32[256,256]{1,0:T(8,128)}, f32[256,64]{1,0:T(8,128)})) %all-reduce.7.cloned.1.call-update) | async-done | bytes 327696 | tf_op jit(solution)/shard_map/psum | solution.py:58
  575.0 6.7 collective-permute-start.1
  582.9 2.3 collective-permute-start.2
  588.4 3.1 collective-permute-start.5
  591.5 1.6 convolution_subtract_fusion.10
  593.2 2.0 collective-permute-done.5
  596.2 4.6 collective-permute-start.9
  601.1 1.6 collective-permute-done.9
  605.3 3.5 collective-permute-start.7
  610.7 11.7 %cholesky.248 = f32[128,128]{1,0:T(8,128)S(1)} custom-call(f32[128,128]{1,0:T(8,128)S(1)} %cholesky.349), custom_call_target="Cholesky" | custom-call | tf_op jit(solution)/shard_map/jit(cholesky)/cholesky | solution.py:27
  622.4 9.8 %custom-call.27 = f32[1,128,128]{1,2,0:T(8,128)S(1)} custom-call(f32[1,128,128]{2,1,0:T(8,128)S(1)} %get-tuple-element.118), custom_call_target="InvertDiagBlocksLowerTriangular" | custom-call | tf_op jit(solution)/shard_map/jit(cholesky)/cholesky | solution.py:27
  632.7 11.7 %cholesky.265 = f32[128,128]{1,0:T(8,128)S(1)} custom-call(f32[128,128]{1,0:T(8,128)S(1)} %convolution_subtract_fusion.16), custom_call_target="Cholesky" | custom-call | tf_op jit(solution)/shard_map/jit(cholesky)/cholesky | solution.py:27
  647.1 4.2 while.8
  651.3 19.7 %custom-call.28 = f32[2,128,128]{1,2,0:T(8,128)S(1)} custom-call(f32[2,128,128]{2,1,0:T(8,128)S(1)} %get-tuple-element.36), custom_call_target="InvertDiagBlocksLowerTriangular" | custom-call | tf_op jit(solution)/shard_map/jit(_cho_solve)/triangular_solve | solution.py:32
  674.0 2.2 collective-permute-start.6
  676.9 4.2 collective-permute-done.6
  683.4 4.5 collective-permute-start.11
  689.8 11.7 %cholesky.282 = f32[128,128]{1,0:T(8,128)S(1)} custom-call(f32[128,128]{1,0:T(8,128)S(1)} %cholesky.352), custom_call_target="Cholesky" | custom-call | tf_op jit(solution)/shard_map/jit(cholesky)/cholesky | solution.py:27
  701.6 9.8 %custom-call.29 = f32[1,128,128]{1,2,0:T(8,128)S(1)} custom-call(f32[1,128,128]{2,1,0:T(8,128)S(1)} %get-tuple-element.114), custom_call_target="InvertDiagBlocksLowerTriangular" | custom-call | tf_op jit(solution)/shard_map/jit(cholesky)/cholesky | solution.py:27
  711.9 11.7 %cholesky.299 = f32[128,128]{1,0:T(8,128)S(1)} custom-call(f32[128,128]{1,0:T(8,128)S(1)} %convolution_subtract_fusion.15), custom_call_target="Cholesky" | custom-call | tf_op jit(solution)/shard_map/jit(cholesky)/cholesky | solution.py:27
  726.3 4.5 while.9
  730.8 19.7 %custom-call.30 = f32[2,128,128]{1,2,0:T(8,128)S(1)} custom-call(f32[2,128,128]{2,1,0:T(8,128)S(1)} %get-tuple-element.37), custom_call_target="InvertDiagBlocksLowerTriangular" | custom-call | tf_op jit(solution)/shard_map/jit(_cho_solve)/triangular_solve | solution.py:32
  752.9 1.8 fusion.25
  754.7 2.5 collective-permute-start.10
  758.1 1.6 convolution_subtract_fusion.2
  759.7 3.6 collective-permute-done.10
  768.6 11.7 %cholesky.316 = f32[128,128]{1,0:T(8,128)S(1)} custom-call(f32[128,128]{1,0:T(8,128)S(1)} %cholesky.355), custom_call_target="Cholesky" | custom-call | tf_op jit(solution)/shard_map/jit(cholesky)/cholesky | solution.py:27
  780.3 9.8 %custom-call.31 = f32[1,128,128]{1,2,0:T(8,128)S(1)} custom-call(f32[1,128,128]{2,1,0:T(8,128)S(1)} %get-tuple-element.110), custom_call_target="InvertDiagBlocksLowerTriangular" | custom-call | tf_op jit(solution)/shard_map/jit(cholesky)/cholesky | solution.py:27
  790.6 11.9 %cholesky.333 = f32[128,128]{1,0:T(8,128)S(1)} custom-call(f32[128,128]{1,0:T(8,128)S(1)} %convolution_subtract_fusion.14), custom_call_target="Cholesky" | custom-call | tf_op jit(solution)/shard_map/jit(cholesky)/cholesky | solution.py:27
  805.3 4.1 while.10
  809.4 19.7 %custom-call.32 = f32[2,128,128]{1,2,0:T(8,128)S(1)} custom-call(f32[2,128,128]{2,1,0:T(8,128)S(1)} %get-tuple-element.38), custom_call_target="InvertDiagBlocksLowerTriangular" | custom-call | tf_op jit(solution)/shard_map/jit(_cho_solve)/triangular_solve | solution.py:32
  831.7 1.6 copy.39
  833.3 2.3 convolution_bitcast_fusion
  (203 shorter events, 70.1 us)
Async XLA Ops:
  7.2 89.2 %all-gather.3.cloned.1.call-start = ((), (), s32[]{:S(2)}) async-start(), calls=%async_computation | async-start | bytes 2129920 | tf_op jit(solution)/shard_map/all_gather | solution.py:40
  7.9 190.2 %all-gather.5.cloned.1.call-start = ((), (), s32[]{:S(2)}) async-start(), calls=%async_computation.1 | async-start | bytes 8519680 | tf_op jit(solution)/shard_map/all_gather | solution.py:43
  8.6 346.3 %all-reduce.5.cloned.1.call-start = ((), (), s32[]{:S(2)}) async-start(), calls=%async_computation.2 | async-start | bytes 524288 | tf_op jit(solution)/shard_map/psum | solution.py:54
  10.8 577.6 %collective-permute-start = (f32[256]{0:T(256)S(1)}, f32[256]{0:T(256)S(1)}, u32[]{:S(2)}, u32[]{:S(2)}) collective-permute-start(f32[256]{0:T(256)S(1)} %fusion.116), channel_id=1, source_target_pairs={{0,64},{64,0},{128,192},{192,128},{256,320},{320,256},{384,448},{4... | collective-permute-start | bytes 3080 | tf_op jit(solution)/shard_map/ppermute | solution.py:12
  20.2 584.3 %collective-permute-start.4 = (f32[256]{0:T(256)S(1)}, f32[256]{0:T(256)S(1)}, u32[]{:S(2)}, u32[]{:S(2)}) collective-permute-start(f32[256]{0:T(256)S(1)} %compare_convert_fusion.2), channel_id=1, source_target_pairs={{0,128},{64,192},{128,0},{192,64},{256,384},{320,448},{384,256},{4... | collective-permute-start | bytes 3080 | tf_op jit(solution)/shard_map/ppermute | solution.py:12
  22.8 659.8 %collective-permute-start.8 = (f32[256]{0:T(256)S(1)}, f32[256]{0:T(256)S(1)}, u32[]{:S(2)}, u32[]{:S(2)}) collective-permute-start(f32[256]{0:T(256)S(1)} %compare_convert_fusion.1), channel_id=1, source_target_pairs={{0,256},{64,320},{128,384},{192,448},{256,0},{320,64},{384,128},{4... | collective-permute-start | bytes 3080 | tf_op jit(solution)/shard_map/ppermute | solution.py:12
  98.5 110.5 %copy-start.2 = (bf16[256,64]{0,1:T(8,128)(2,1)S(1)}, bf16[256,64]{0,1:T(8,128)(2,1)}, u32[]{:S(2)}) copy-start(bf16[256,64]{0,1:T(8,128)(2,1)} %param.13) | copy-start | bytes 98308
  206.9 215.8 %copy-start.1 = (bf16[256,256]{1,0:T(8,128)(2,1)S(1)}, bf16[256,256]{1,0:T(8,128)(2,1)}, u32[]{:S(2)}) copy-start(bf16[256,256]{1,0:T(8,128)(2,1)} %param.14) | copy-start | bytes 393220
  208.7 366.2 %all-reduce.7.cloned.1.call-start = ((), (), s32[]{:S(2)}) async-start(), calls=%async_computation.3 | async-start | bytes 786432 | tf_op jit(solution)/shard_map/psum | solution.py:58
  354.9 69.6 %copy-start = (f32[256,256]{1,0:T(8,128)S(1)}, f32[256,256]{1,0:T(8,128)}, u32[]{:S(2)}) copy-start(f32[256,256]{1,0:T(8,128)} %all-reduce.5.cloned.1.call-done) | copy-start | bytes 786436
  424.5 166.9 %collective-permute-start.3 = (f32[256,256]{1,0:T(8,128)S(1)}, f32[256,256]{1,0:T(8,128)S(1)}, u32[]{:S(2)}, u32[]{:S(2)}) collective-permute-start(f32[256,256]{1,0:T(8,128)S(1)} %copy-done), channel_id=1, source_target_pairs={{0,64},{64,0},{128,192},{192,128},{256,320},{320,256},{384,448},{4... | collective-permute-start | bytes 786440 | tf_op jit(solution)/shard_map/ppermute | solution.py:12
  575.0 7.9 collective-permute-start.1
  582.9 20.1 %collective-permute-start.2 = (f32[256,256]{1,0:T(8,128)}, f32[256,256]{1,0:T(8,128)S(1)}, u32[]{:S(2)}, u32[]{:S(2)}) collective-permute-start(f32[256,256]{1,0:T(8,128)} %get-tuple-element.87), channel_id=1, source_target_pairs={{0,64},{64,0},{128,192},{192,128},{256,320},{320,256},{384,448},{4... | collective-permute-start | bytes 786440 | tf_op jit(solution)/shard_map/ppermute | solution.py:12
  588.4 6.8 collective-permute-start.5
  596.2 6.5 collective-permute-start.9
  600.9 72.5 %copy-start.3 = (f32[256,256]{1,0:T(8,128)S(1)}, f32[256,256]{1,0:T(8,128)}, u32[]{:S(2)}) copy-start(f32[256,256]{1,0:T(8,128)} %get-tuple-element.87) | copy-start | bytes 786436
  605.3 71.0 %collective-permute-start.7 = (f32[256,256]{1,0:T(8,128)S(1)}, f32[256,256]{1,0:T(8,128)S(1)}, u32[]{:S(2)}, u32[]{:S(2)}) collective-permute-start(f32[256,256]{1,0:T(8,128)S(1)} %get-tuple-element.96), channel_id=1, source_target_pairs={{0,128},{64,192},{128,0},{192,64},{256,384},{320,448},{384,256},{4... | collective-permute-start | bytes 786440 | tf_op jit(solution)/shard_map/ppermute | solution.py:12
  674.0 2.9 copy-start.4
  674.0 7.1 collective-permute-start.6
  681.1 2.3 copy-start.5
  683.4 74.7 %collective-permute-start.11 = (f32[256,256]{1,0:T(8,128)S(1)}, f32[256,256]{1,0:T(8,128)}, u32[]{:S(2)}, u32[]{:S(2)}) collective-permute-start(f32[256,256]{1,0:T(8,128)S(1)} %get-tuple-element.92), channel_id=1, source_target_pairs={{0,256},{64,320},{128,384},{192,448},{256,0},{320,64},{384,128},{4... | collective-permute-start | bytes 786440 | tf_op jit(solution)/shard_map/ppermute | solution.py:12
  754.7 8.7 %collective-permute-start.10 = (f32[256,256]{1,0:T(8,128)S(1)}, f32[256,256]{1,0:T(8,128)}, u32[]{:S(2)}, u32[]{:S(2)}) collective-permute-start(f32[256,256]{1,0:T(8,128)S(1)} %fusion.25), channel_id=1, source_target_pairs={{0,256},{64,320},{128,384},{192,448},{256,0},{320,64},{384,128},{4... | collective-permute-start | bytes 786440 | tf_op jit(solution)/shard_map/ppermute | solution.py:12
Sparse Core Ops, SparseCore 0:
  11.0 85.3 all-gather.2
  99.4 98.6 all-gather.4
  208.9 146.0 all-reduce.4
  423.8 151.1 all-reduce.6
where the time goes:
time: 852 us; the launch traced here: 842 us
  waiting for transfers between devices  468 us (55%)
  other arithmetic  235 us (28%)
  starting transfers between devices  49 us (6%)
  matrix products  38.8 us (5%)
  local copies, waits for them, and re-layouts  28.2 us (3%)
  between operations  23 us (3%)
    psum x1, waiting for transfers between devices, shards(): picked, chosen = lax.psum((part_rows, part_points), 'sub')  144 us
    psum x1, waiting for transfers between devices, shards(): compressed = lax.psum(local_part, 'sub')  144 us
    another operation x27, other arithmetic, factorize(): jnp.linalg.cholesky(gram + shift * jnp.eye(picked.shape[0], dtype=jnp.flo...  138 us
    all_gather x1, waiting for transfers between devices, shards(): lax.all_gather(omega, 'sub', axis=0, tiled=True)  99.6 us
    another operation x9, other arithmetic, interpolate(): return jax.scipy.linalg.cho_solve((factor, True), right_side).T  78.8 us
    all_gather x1, waiting for transfers between devices, shards(): lax.all_gather(points, 'sub', axis=0, tiled=True)  67.4 us
    ppermute x12, starting transfers between devices, partner(): return lax.ppermute(value, axis, pairs)  48.6 us
  transfers between devices with their start and end apart: 16, of which 9 were waited for; matrix products, arithmetic and copies ran while one was open for 27% of the time, Pallas kernels for 0%

commit v1 on v0

v1 whole, which is shorter than its diff:
```python
import jax
import jax.numpy as jnp
from jax import lax
from jax.experimental import pallas as pl
from jax.experimental.pallas import tpu as pltpu
from jax.sharding import PartitionSpec as P

F32 = jnp.float32
BF16 = jnp.bfloat16
RING = 8
N = 256
AUG = 128
CUT = N // RING
LEVELS = 3
OWN = RING // 2 - 1
NN = ((1,), (0,))
NT = ((1,), (1,))
TN = ((0,), (0,))
DEAD = -1e30
MESH = pl.DeviceIdType.MESH

SPAN = N + 1.0
SIGMA = (SPAN + 1.0) / (SPAN - 1.0)
CHEB = 2.0 * SIGMA * SIGMA - 1.0
ALPHA = 8.0 * (SPAN + 1.0) / ((SPAN - 1.0) ** 2 * CHEB)
BETA = 8.0 / ((SPAN - 1.0) ** 2 * CHEB)
RATES = []
RHO = 1.0 / CHEB
for _ in range(6):
    RATES.append(2.0 / (2.0 - RHO * RHO))
    RHO = RHO * RHO / (2.0 - RHO * RHO)


def bdot(a, b, dims=NN):
    return lax.dot_general(a, b, (dims, ((), ())), preferred_element_type=F32)


def split2(x):
    hi = x.astype(BF16)
    return hi, (x - hi.astype(F32)).astype(BF16)


def split3(x):
    hi = x.astype(BF16)
    rest = x - hi.astype(F32)
    mid = rest.astype(BF16)
    return hi, mid, (rest - mid.astype(F32)).astype(BF16)


def dot3(a, b, dims=NN):
    ah, al = split2(a)
    bh, bl = split2(b)
    return bdot(ah, bh, dims) + (bdot(ah, bl, dims) + bdot(al, bh, dims))


def pick(onehot, x, dims=NN):
    hi, mid, lo = split3(x)
    return bdot(onehot, hi, dims) + bdot(onehot, mid, dims) + bdot(onehot, lo, dims)


def dot6(a, b, dims=NN):
    return lax.dot_general(
        a, b, (dims, ((), ())), precision=lax.Precision.HIGHEST, preferred_element_type=F32
    )


def iota(shape, dim):
    return lax.broadcasted_iota(jnp.int32, shape, dim)


def ridge_inverse(p):
    gram = dot6(p, p, NT)
    inv_shift = 1.0 / (jnp.sum(p * p) / N + 1e-06)
    eye = (iota((N, N), 0) == iota((N, N), 1)).astype(F32)
    b = gram * inv_shift + eye
    x = ALPHA * eye - BETA * b
    e = eye - dot3(b, x)
    for w in RATES:
        eh, el = split2(e)
        xh, xl = split2(x)
        e2 = bdot(eh, eh) + (bdot(eh, el) + bdot(el, eh))
        x = w * (x + (bdot(xh, eh) + (bdot(xh, el) + bdot(xl, eh))))
        e = (1.0 - w) * eye + w * e2
    x = x + dot6(x, eye - dot6(b, x))
    return x * inv_shift


def gauss(left_f, right_g):
    return jnp.exp(bdot(left_f, right_g, NT) * 0.0625)


def body(
    omega_ref, points_ref, samples_ref, skel_ref, mskel_ref, ranks_ref,
    leaf_out, node_out, coup_out, top_out,
    zbuf, ybuf, tot, rsb, base,
    csp, crz, csum, cry, cz, och, xch,
    psp, prz, psum, pry, opk, xpk,
    mtp, mr1, ms1, mr2, mfull, ocm, xcm, onehots, cy, co,
    send_sem, recv_sem,
):
    sub = lax.axis_index("sub")
    leaf = lax.axis_index("leaf")
    z = sub // RING
    y = sub % RING

    def zpeer(d):
        return {"sub": lax.rem(z + d + RING, RING) * RING + y}

    def ypeer(d):
        return {"sub": z * RING + lax.rem(y + d + RING, RING)}

    barrier = pltpu.get_barrier_semaphore()
    for d in range(1, RING):
        pl.semaphore_signal(barrier, inc=1, device_id=zpeer(d), device_id_type=MESH)
        pl.semaphore_signal(barrier, inc=1, device_id=ypeer(d), device_id_type=MESH)
    partners = []
    for level in range(LEVELS):
        bit = (leaf // 2**level) % 2
        partners.append({"leaf": leaf + (1 - 2 * bit) * 2**level})
        pl.semaphore_signal(barrier, inc=1, device_id=partners[-1], device_id_type=MESH)

    copies = []

    def send(src, dst, device):
        at = len(copies)
        copy = pltpu.make_async_remote_copy(
            src_ref=src, dst_ref=dst, send_sem=send_sem.at[at], recv_sem=recv_sem.at[at],
            device_id=device, device_id_type=MESH,
        )
        copy.start()
        copies.append(copy)
        return copy

    def arrive(group):
        for copy in group:
            copy.wait_recv()

    base[...] = jnp.zeros((N, AUG), F32)
    pts = points_ref[...].astype(F32)
    base[:, :64] = pts
    half = -0.5 * jnp.sum(pts * pts, axis=1, keepdims=True)
    h1, h2, h3 = (piece.astype(F32) for piece in split3(half))
    lane = iota((N, AUG), 1)
    plain = base[...]

    def place(at, other):
        out = jnp.where((lane >= other) & (lane < other + 3), 1.0, plain)
        for i, piece in enumerate((h1, h2, h3)):
            out = jnp.where(lane == at + i, piece, out)
        return out.astype(BF16)

    feat = place(64, 67)
    omega = omega_ref[...]
    samples = samples_ref[...]
    eye = (iota((N, N), 0) == iota((N, N), 1)).astype(BF16)
    omega_t = bdot(eye, omega, NT).astype(BF16)
    zbuf[OWN, :, :N] = omega
    zbuf[OWN, :, N:] = place(67, 64)
    ybuf[OWN, :, :N] = omega_t
    ybuf[OWN, :, N:] = feat
    column = iota((1, N), 1)
    offset = skel_ref[...] - sub * N
    hits = (iota((N, N), 0) == offset) & (column < ranks_ref[0, 0])
    hits = hits.astype(F32).astype(BF16)
    hot = bdot(eye, hits, NT).astype(BF16)
    csp[...] = bdot(hot, feat).astype(BF16)

    pl.semaphore_wait(barrier, 2 * (RING - 1) + LEVELS)

    def scatter(src, dst, peer, pos, rows):
        group = []
        for d in range(1, RING):
            to = lax.rem(pos + d, RING)
            group.append(
                send(src.at[pl.ds(pl.multiple_of(to * rows, rows), rows)], dst.at[d], peer(d))
            )
        return group

    def spread(src, dst, peer):
        return [send(src, dst.at[d], peer(d)) for d in range(1, RING)]

    def own_rows(pos, rows):
        return pl.ds(pl.multiple_of(pos * rows, rows), rows)

    def gather(full, peer, pos, rows, start=0):
        at = pl.ds(pl.multiple_of(start + pos * rows, rows), rows)
        return [send(full.at[at], full.at[at], peer(d)) for d in range(1, RING)]

    chosen_rs = scatter(csp, crz, zpeer, z, CUT)

    def ring_step(buf, peer, s):
        if s < 4:
            right = send(buf.at[OWN + s - 1], buf.at[OWN + s], peer(1))
            left = send(buf.at[OWN - s + 1], buf.at[OWN - s], peer(-1))
        else:
            half_rows = N // 2
            right = send(
                buf.at[OWN + 3, pl.ds(0, half_rows)], buf.at[OWN + 4, pl.ds(0, half_rows)], peer(1)
            )
            left = send(
                buf.at[OWN - 3, pl.ds(half_rows, half_rows)],
                buf.at[OWN + 4, pl.ds(half_rows, half_rows)],
                peer(-1),
            )
        return [right, left]

    flying = ring_step(zbuf, zpeer, 1) + ring_step(ybuf, ypeer, 1)
    psp[...] = pick(hot, samples)
    picked_rs = scatter(psp, prz, zpeer, z, CUT)

    def block(r, c, first):
        weights = gauss(ybuf[r, :, N:], zbuf[c, :, N:]).astype(BF16)
        term = bdot(weights, zbuf[c, :, :N])
        if first:
            tot[r] = term
        else:
            tot[r] += term

    is_upper = [(leaf // 2**level) % 2 for level in range(LEVELS)]
    for level in range(LEVELS):
        index = mskel_ref[pl.ds(level, 1), :]
        index = lax.rem(index + N * is_upper[level], 2 * N)
        wide = (iota((2 * N, N), 0) == index) & (column < ranks_ref[0, level + 1])
        onehots[level] = bdot(eye, wide.astype(F32).astype(BF16), NT).astype(BF16)

    def dead_rows(x, row0, rank):
        rows = x.shape[0]
        gone = iota((rows, AUG), 0) + row0 >= rank
        at = iota((rows, AUG), 1)
        x = jnp.where(gone & (at == 64), DEAD, x)
        return jnp.where(gone & (at == 67), 1.0, x).astype(BF16)

    seen = set()
    known = [OWN]
    for s in range(5):
        if s > 0:
            arrive(flying)
            known = list(range(max(0, OWN - s), OWN + s + 1))
        if s < 4:
            flying = ring_step(zbuf, zpeer, s + 1) + ring_step(ybuf, ypeer, s + 1) if s > 0 else flying
        if s == 1:
            arrive(chosen_rs)
            total = csp[own_rows(z, CUT), :].astype(F32)
            for d in range(1, RING):
                total += crz[d].astype(F32)
            csum[...] = total.astype(BF16)
            chosen_ag = spread(csum, cry, ypeer)
        if s == 2:
            arrive(chosen_ag)
            total = csum[...].astype(F32)
            for d in range(1, RING):
                total += cry[d].astype(F32)
            cz[...] = dead_rows(total, z * CUT, ranks_ref[0, 0])
            och[0, own_rows(z, CUT), :] = cz[...]
            chosen_all = gather(och.at[0], zpeer, z, CUT)
        if s == 4:
            arrive(picked_rs)
            total = psp[own_rows(z, CUT), :]
            for d in range(1, RING):
                total += prz[d]
            for c in range(RING):
                weights = gauss(cz[...], zbuf[c, :, N:]).astype(BF16)
                total -= bdot(weights, zbuf[c, :, :N])
            psum[...] = total
            picked_ag = spread(psum, pry, ypeer)
        for c in known:
            for r in known:
                if (r, c) not in seen:
                    block(r, c, all((r, k) not in seen for k in range(RING)))
                    seen.add((r, c))

    sh, sl = split2(samples)
    mt = bdot(omega_t, sh) + bdot(omega_t, sl)
    for r in range(RING):
        th, tl = split2(tot[r])
        turned = ybuf[r, :, :N]
        mt -= bdot(turned, th) + bdot(turned, tl)
    mtp[...] = mt
    halves = ((0, z, zpeer, ypeer), (N // 2, y, ypeer, zpeer))
    piece = N // 2 // RING
    stage = []
    for i, (start, pos, first, second) in enumerate(halves):
        stage += scatter(mtp.at[pl.ds(start, N // 2)], mr1.at[i], first, pos, piece)

    arrive(picked_ag)
    total = psum[...]
    for d in range(1, RING):
        total += pry[d]
    opk[0, own_rows(z, CUT), :] = total
    picked_all = gather(opk.at[0], zpeer, z, CUT)

    arrive(stage)
    stage = []
    for i, (start, pos, first, second) in enumerate(halves):
        at = pl.ds(pl.multiple_of(start + pos * piece, piece), piece)
        total = mtp[at, :]
        for d in range(1, RING):
            total += mr1[i, d]
        ms1[i] = total
        stage += spread(ms1.at[i], mr2.at[i], second)
    arrive(stage)
    stage = []
    for i, (start, pos, first, second) in enumerate(halves):
        total = ms1[i]
        for d in range(1, RING):
            total += mr2[i, d]
        at = pl.ds(pl.multiple_of(start + pos * piece, piece), piece)
        mfull[at, :] = total
        stage += gather(mfull, first, pos, piece, start)

    arrive(chosen_all)
    arrive(picked_all)

    def swap(level):
        return [
            send(och.at[level], xch.at[level], partners[level]),
            send(opk.at[level], xpk.at[level], partners[level]),
        ]

    early = swap(0)

    hr = N // 2
    flows = []

    def sum_step(s):
        if s > 0:
            arrive(flows[-1])
            if s == 1:
                tot[OWN - 3, :hr] += rsb[0, 0, :hr]
                tot[OWN + 3, hr:] += rsb[1, 0, hr:]
            else:
                tot[OWN - 4 + s] += rsb[0, s - 1]
                tot[OWN + 4 - s] += rsb[1, s - 1]
        if s == 0:
            lower, upper = pl.ds(0, hr), pl.ds(hr, hr)
            flows.append([
                send(tot.at[OWN + 4, lower], rsb.at[0, 0, lower], ypeer(1)),
                send(tot.at[OWN + 4, upper], rsb.at[1, 0, upper], ypeer(-1)),
            ])
        elif s < 4:
            flows.append([
                send(tot.at[OWN - 4 + s], rsb.at[0, s], ypeer(1)),
                send(tot.at[OWN + 4 - s], rsb.at[1, s], ypeer(-1)),
            ])

    sum_step(0)
    picked = opk[0]
    inverse = ridge_inverse(picked)
    turned_leaf = dot3(inverse, picked)
    arrive(stage)
    ocm[0] = dot6(inverse, dot6(picked, mfull[...], NT))
    late = send(ocm.at[0], xcm.at[0], partners[0])

    row = iota((AUG, AUG), 0)
    col = iota((AUG, AUG), 1)
    turn = jnp.where((row >= 64) & (row < 67), row + 3, jnp.where((row >= 67) & (row < 70), row - 3, row))
    turn = (turn == col).astype(F32).astype(BF16)

    for level in range(1, LEVELS + 1):
        last = level - 1
        sum_step(level)
        early[0].wait_recv()
        own_f, other_f = och[last], xch[last]
        own_g = bdot(own_f, turn).astype(BF16)
        other_g = bdot(other_f, turn).astype(BF16)
        coupling = gauss(own_f, other_g)
        coupling_t = gauss(other_f, own_g)
        coup_out[0, last] = coupling
        onehot = onehots[last]
        fresh = bdot(onehot[:, :N], own_f) + bdot(onehot[:, N:], other_f)
        och[level] = dead_rows(fresh, 0, ranks_ref[0, level])
        if level == LEVELS:
            sum_step(4)
            resid = samples_ref[...] - tot[OWN]
            leaf_out[...] = dot3(resid, turned_leaf, NT)
        early[1].wait_recv()
        late.wait_recv()
        co[:N] = ocm[last]
        co[N:] = xcm[last]
        cy[:N] = opk[last] - dot3(coupling, xcm[last])
        cy[N:] = xpk[last] - dot3(coupling_t, ocm[last])
        cand = cy[...]
        picked = pick(onehot, cand)
        opk[level] = picked
        if level < LEVELS:
            early = swap(level)
        inverse = ridge_inverse(picked)
        weight = dot6(dot6(picked, cand, NT), co[...])
        compressed = dot6(inverse, weight)
        if level < LEVELS:
            ocm[level] = compressed
            late = send(ocm.at[level], xcm.at[level], partners[level])
        else:
            top_out[0] = compressed
        interp = dot3(cand, dot3(inverse, picked), NT)
        at = is_upper[last] * N
        node_out[0, last, pl.ds(pl.multiple_of(at, N), N), :] = interp[:N]
        node_out[0, last, pl.ds(pl.multiple_of(N - at, N), N), :] = interp[N:]

    for copy in copies:
        copy.wait_send()


N_COPIES = 16 + 6 * (RING - 1) + 6 * (RING - 1) + 8 + 3 * LEVELS


def shards(points, omega, samples, ranks, leaf_skeleton, merge_skeleton):
    vmem = pl.BlockSpec(memory_space=pltpu.VMEM)
    return pl.pallas_call(
        body,
        out_shape=(
            jax.ShapeDtypeStruct((N, N), F32),
            jax.ShapeDtypeStruct((1, LEVELS, 2 * N, N), F32),
            jax.ShapeDtypeStruct((1, LEVELS, N, N), F32),
            jax.ShapeDtypeStruct((1, N, N), F32),
        ),
        in_specs=[vmem] * 5 + [pl.BlockSpec(memory_space=pltpu.SMEM)],
        out_specs=(vmem,) * 4,
        scratch_shapes=[
            pltpu.VMEM((RING, N, N + AUG), BF16),
            pltpu.VMEM((RING, N, N + AUG), BF16),
            pltpu.VMEM((RING, N, N), F32),
            pltpu.VMEM((2, 4, N, N), F32),
            pltpu.VMEM((N, AUG), F32),
            pltpu.VMEM((N, AUG), BF16),
            pltpu.VMEM((RING, CUT, AUG), BF16),
            pltpu.VMEM((CUT, AUG), BF16),
            pltpu.VMEM((RING, CUT, AUG), BF16),
            pltpu.VMEM((CUT, AUG), BF16),
            pltpu.VMEM((LEVELS + 1, N, AUG), BF16),
            pltpu.VMEM((LEVELS, N, AUG), BF16),
            pltpu.VMEM((N, N), F32),
            pltpu.VMEM((RING, CUT, N), F32),
            pltpu.VMEM((CUT, N), F32),
            pltpu.VMEM((RING, CUT, N), F32),
            pltpu.VMEM((LEVELS + 1, N, N), F32),
            pltpu.VMEM((LEVELS, N, N), F32),
            pltpu.VMEM((N, N), F32),
            pltpu.VMEM((2, RING, CUT // 2, N), F32),
            pltpu.VMEM((2, CUT // 2, N), F32),
            pltpu.VMEM((2, RING, CUT // 2, N), F32),
            pltpu.VMEM((N, N), F32),
            pltpu.VMEM((LEVELS, N, N), F32),
            pltpu.VMEM((LEVELS, N, N), F32),
            pltpu.VMEM((LEVELS, N, 2 * N), BF16),
            pltpu.VMEM((2 * N, N), F32),
            pltpu.VMEM((2 * N, N), F32),
            pltpu.SemaphoreType.DMA((N_COPIES,)),
            pltpu.SemaphoreType.DMA((N_COPIES,)),
        ],
        compiler_params=pltpu.CompilerParams(
            collective_id=0, has_side_effects=True, vmem_limit_bytes=56 * 2**20
        ),
    )(omega, points, samples, leaf_skeleton, merge_skeleton[0], ranks)


def solution(mesh):
    in_specs = (
        P(("leaf", "sub"), None),
        P(("leaf", "sub"), None),
        P(("leaf", "sub"), None),
        P("leaf", None),
        P("leaf", None),
        P("leaf", None, None),
    )
    out_specs = (
        P(("leaf", "sub"), None),
        P("leaf", None, None, None),
        P("leaf", None, None, None),
        P("leaf", None, None),
    )
    return jax.shard_map(shards, mesh=mesh, in_specs=in_specs, out_specs=out_specs, check_vma=False)
```

time: 852 us -> 135 us (0.16); the launches traced: 842 us -> 134 us
  waiting for transfers between devices: 468 us -> 0 us
  other arithmetic: 235 us -> 0 us
  Pallas kernels: 0 us -> 125 us
  starting transfers between devices: 49 us -> 0 us
  matrix products: 38.8 us -> 0 us
  between operations: 23 us -> 0.64 us
  local copies, waits for them, and re-layouts: 28.2 us -> 8.77 us
    psum x2 -> x0, waiting for transfers between devices: 288 us -> none  [the longest x1 144 us: shards(): picked, chosen = lax.psum((part_rows, part_points), 'sub')]
    another operation x40 -> x0, other arithmetic: 217 us -> none  [the longest x27 138 us: factorize(): jnp.linalg.cholesky(gram + shift * jnp.eye(picked.shape[0], dtype=jnp.flo...]
    all_gather x2 -> x0, waiting for transfers between devices: 167 us -> none  [the longest x1 99.6 us: shards(): lax.all_gather(omega, 'sub', axis=0, tiled=True)]
    pallas_call x0 -> x1, Pallas kernels: none -> 125 us  [shards(): pl.pallas_call(body, out_shape=(jax.ShapeDtypeStruct((N, N), F32), jax.Sh...]
    ppermute x12 -> x0, starting transfers between devices: 48.6 us -> none  [partner(): return lax.ppermute(value, axis, pairs)]
    dot_general x22 -> x0, matrix products: 28.1 us -> none  [the longest x1 8.74 us: shards(): jnp.dot(weights, lax.all_gather(omega, 'sub', axis=0, tiled=True), prefer...]
    another operation x42 -> x0, local copies, waits for them, and re-layouts: 16.7 us -> none  [the longest x19 12.1 us: interpolate(): return jax.scipy.linalg.cho_solve((factor, True), right_side).T]
    ppermute x12 -> x0, waiting for transfers between devices: 11.6 us -> none  [partner(): return lax.ppermute(value, axis, pairs)]
  transfers between devices with their start and end apart: 16 -> 0, of which waited for: 9 -> 0; matrix products, arithmetic and copies ran while one was open for 27% -> 0% of each run, Pallas kernels for 0% -> 0%
where the time goes in v1:
time: 135 us; the launch traced here: 134 us
  Pallas kernels  125 us (93%)
  local copies, waits for them, and re-layouts  8.77 us (6%)
    pallas_call x1, Pallas kernels, shards(): pl.pallas_call(body, out_shape=(jax.ShapeDtypeStruct((N, N), F32), jax.Sh...  125 us
    unnamed x10, local copies, waits for them, and re-layouts  8.77 us

profile of v1, /device:TPU:1, one launch (start us, length us, event | category | flops | bytes accessed | tf_op | source)
XLA Modules:
  0.0 134.4 jit_solution(2876362236414236108)
XLA Ops:
  0.6 1.3 copy.13
  1.9 1.5 %copy.10.points_ref = bf16[256,64]{1,0:T(8,128)(2,1)} copy(bf16[256,64]{0,1:T(8,128)(2,1)} %param.6) | data formatting | bytes 65536 | tf_op args[0]
  3.4 125.0 %shard_map.93 = (f32[256,256]{1,0:T(8,128)}, f32[1,3,512,256]{3,2,1,0:T(8,128)}, f32[1,3,256,256]{3,2,1,0:T(8,128)}, f32[1,256,256]{2,1,0:T(8,128)}) custom-call(bf16[256,256]{1,0:T(8,128)(2,1)} %omega_ref.1, bf16[256,64]{1,0:T(8,128)(2,1)} %copy.10.points_ref, f32[256,256]{1,0:T(8,128)} %samples_ref.1, s32[1,256]{1,0:T(1,128)} %skel_ref.1, ...), custom_call_target="tpu_custom_call" | custom-call | tf_op jit(solution)/shard_map/pallas_call | solution.py:409
  128.4 1.7 %copy.18 = f32[256,256]{1,0:T(8,128)} copy(f32[256,256]{1,0:T(8,128)} %get-tuple-element.8) | data formatting | bytes 524288
  130.1 0.0 copy-start
  130.1 0.0 copy-start.1
  130.1 2.7 %copy.19 = f32[1,3,512,256]{3,2,1,0:T(8,128)} copy(f32[1,3,512,256]{3,2,1,0:T(8,128)} %get-tuple-element.9) | data formatting | bytes 3145728
  132.8 0.0 copy-done
  132.8 0.9 copy.20
  133.7 0.0 copy-done.1
  133.7 0.7 copy.21
Async XLA Ops:
  130.1 2.7 %copy-start = (f32[1,3,256,256]{3,2,1,0:T(8,128)S(1)}, f32[1,3,256,256]{3,2,1,0:T(8,128)}, u32[]{:S(2)}) copy-start(f32[1,3,256,256]{3,2,1,0:T(8,128)} %get-tuple-element.10) | copy-start | bytes 2359300
  130.1 3.6 %copy-start.1 = (f32[1,256,256]{2,1,0:T(8,128)S(1)}, f32[1,256,256]{2,1,0:T(8,128)}, u32[]{:S(2)}) copy-start(f32[1,256,256]{2,1,0:T(8,128)} %get-tuple-element.11) | copy-start | bytes 786436

commit v2 on v1

v2 whole, which is shorter than its diff:
```python
import jax
import jax.numpy as jnp
from jax import lax
from jax.experimental import pallas as pl
from jax.experimental.pallas import tpu as pltpu
from jax.sharding import PartitionSpec as P

F32 = jnp.float32
BF16 = jnp.bfloat16
RING = 8
N = 256
AUG = 128
CUT = N // RING
LEVELS = 3
OWN = RING // 2 - 1
NN = ((1,), (0,))
NT = ((1,), (1,))
TN = ((0,), (0,))
DEAD = -1e30
MESH = pl.DeviceIdType.MESH

SPAN = N + 1.0
SIGMA = (SPAN + 1.0) / (SPAN - 1.0)
CHEB = 2.0 * SIGMA * SIGMA - 1.0
ALPHA = 8.0 * (SPAN + 1.0) / ((SPAN - 1.0) ** 2 * CHEB)
BETA = 8.0 / ((SPAN - 1.0) ** 2 * CHEB)
RATES = []
RHO = 1.0 / CHEB
for _ in range(6):
    RATES.append(2.0 / (2.0 - RHO * RHO))
    RHO = RHO * RHO / (2.0 - RHO * RHO)


def bdot(a, b, dims=NN):
    return lax.dot_general(a, b, (dims, ((), ())), preferred_element_type=F32)


def split2(x):
    hi = x.astype(BF16)
    return hi, (x - hi.astype(F32)).astype(BF16)


def split3(x):
    hi = x.astype(BF16)
    rest = x - hi.astype(F32)
    mid = rest.astype(BF16)
    return hi, mid, (rest - mid.astype(F32)).astype(BF16)


def dot3(a, b, dims=NN):
    ah, al = split2(a)
    bh, bl = split2(b)
    return bdot(ah, bh, dims) + (bdot(ah, bl, dims) + bdot(al, bh, dims))


def pick(onehot, x, dims=NN):
    hi, mid, lo = split3(x)
    return bdot(onehot, hi, dims) + bdot(onehot, mid, dims) + bdot(onehot, lo, dims)


def dot6(a, b, dims=NN):
    return lax.dot_general(
        a, b, (dims, ((), ())), precision=lax.Precision.HIGHEST, preferred_element_type=F32
    )


def iota(shape, dim):
    return lax.broadcasted_iota(jnp.int32, shape, dim)


def ridge_inverse(p):
    gram = dot6(p, p, NT)
    inv_shift = 1.0 / (jnp.sum(p * p) / N + 1e-06)
    eye = (iota((N, N), 0) == iota((N, N), 1)).astype(F32)
    b = gram * inv_shift + eye
    x = ALPHA * eye - BETA * b
    e = eye - dot3(b, x)
    for w in RATES:
        eh, el = split2(e)
        xh, xl = split2(x)
        e2 = bdot(eh, eh) + (bdot(eh, el) + bdot(el, eh))
        x = w * (x + (bdot(xh, eh) + (bdot(xh, el) + bdot(xl, eh))))
        e = (1.0 - w) * eye + w * e2
    x = x + dot6(x, eye - dot6(b, x))
    return x * inv_shift


def gauss(left_f, right_g):
    return jnp.exp(bdot(left_f, right_g, NT) * 0.0625)


def body(
    omega_ref, points_ref, samples_ref, skel_ref, mskel_ref, ranks_ref,
    diag_out, turn_out, node_out, coup_out, top_out,
    zbuf, ybuf, tot, rsb,
    csp, crz, cry, cz, och, xch,
    psp, prz, pry, opk, xpk,
    mtp, mr1, mr2, mfull, ocm, xcm, onehots, cy, co,
    send_sem, recv_sem,
):
    sub = lax.axis_index("sub")
    leaf = lax.axis_index("leaf")
    z = sub // RING
    y = sub % RING

    def zpeer(d):
        return {"sub": lax.rem(z + d + RING, RING) * RING + y}

    def ypeer(d):
        return {"sub": z * RING + lax.rem(y + d + RING, RING)}

    barrier = pltpu.get_barrier_semaphore()
    for d in range(1, RING):
        pl.semaphore_signal(barrier, inc=1, device_id=zpeer(d), device_id_type=MESH)
        pl.semaphore_signal(barrier, inc=1, device_id=ypeer(d), device_id_type=MESH)
    partners = []
    for level in range(LEVELS):
        bit = (leaf // 2**level) % 2
        partners.append({"leaf": leaf + (1 - 2 * bit) * 2**level})
        pl.semaphore_signal(barrier, inc=1, device_id=partners[-1], device_id_type=MESH)

    copies = []

    def send(src, dst, device):
        at = len(copies)
        copy = pltpu.make_async_remote_copy(
            src_ref=src, dst_ref=dst, send_sem=send_sem.at[at], recv_sem=recv_sem.at[at],
            device_id=device, device_id_type=MESH,
        )
        copy.start()
        copies.append(copy)
        return copy

    def arrive(group):
        for copy in group:
            copy.wait_recv()

    eye = (iota((N, N), 0) == iota((N, N), 1)).astype(BF16)
    padded = jnp.concatenate([points_ref[...], jnp.zeros((AUG - 64, N), BF16)], axis=0)
    plain = bdot(eye, padded, NT)
    half = -0.5 * jnp.sum(plain * plain, axis=1, keepdims=True)
    h1, h2, h3 = (piece.astype(F32) for piece in split3(half))
    lane = iota((N, AUG), 1)

    def place(at, other):
        out = jnp.where((lane >= other) & (lane < other + 3), 1.0, plain)
        for i, piece in enumerate((h1, h2, h3)):
            out = jnp.where(lane == at + i, piece, out)
        return out.astype(BF16)

    feat = place(64, 67)
    omega = omega_ref[...]
    samples = samples_ref[...]
    omega_t = bdot(eye, omega, NT).astype(BF16)
    zbuf[OWN, :, :N] = omega
    zbuf[OWN, :, N:] = place(67, 64)
    ybuf[OWN, :, :N] = omega_t
    ybuf[OWN, :, N:] = feat
    column = iota((1, N), 1)
    offset = skel_ref[...] - sub * N
    hits = (iota((N, N), 0) == offset) & (column < ranks_ref[0, 0])
    hits = hits.astype(F32).astype(BF16)
    hot = bdot(eye, hits, NT).astype(BF16)
    csp[...] = bdot(hot, feat).astype(BF16)

    pl.semaphore_wait(barrier, 2 * (RING - 1) + LEVELS)

    def scatter(src, dst, peer, pos, rows):
        group = []
        for d in range(1, RING):
            to = lax.rem(pos + d, RING)
            group.append(
                send(src.at[pl.ds(pl.multiple_of(to * rows, rows), rows)], dst.at[d], peer(d))
            )
        return group

    def spread(dst, peer, pos):
        return [send(dst.at[pos], dst.at[pos], peer(d)) for d in range(1, RING)]

    def own_rows(pos, rows):
        return pl.ds(pl.multiple_of(pos * rows, rows), rows)

    def gather(full, peer, pos, rows, start=0):
        at = pl.ds(pl.multiple_of(start + pos * rows, rows), rows)
        return [send(full.at[at], full.at[at], peer(d)) for d in range(1, RING)]

    chosen_rs = scatter(csp, crz, zpeer, z, CUT)

    hr = N // 2
    top, bottom = pl.ds(0, hr), pl.ds(hr, hr)

    def right(axis, s, part):
        buf, peer = axis
        at = top if part == 0 else bottom
        return send(buf.at[OWN + s - 1, at], buf.at[OWN + s, at], peer(1))

    def left(axis, s, part):
        buf, peer = axis
        at = top if part == 0 else bottom
        to = OWN - s if s < 4 else OWN + 4
        return send(buf.at[OWN - s + 1, at], buf.at[to, at], peer(-1))

    axes = ((zbuf, zpeer), (ybuf, ypeer))
    flying = {}

    def launch(axis, s, part):
        if s < 4 or part == 0:
            flying[axis, 0, s, part] = right(axes[axis], s, part)
        if s < 4 or part == 1:
            flying[axis, 1, s, part] = left(axes[axis], s, part)

    for part in range(2):
        for axis in range(2):
            launch(axis, 1, part)

    def block(r, c, first):
        weights = gauss(ybuf[r, :, N:], zbuf[c, :, N:]).astype(BF16)
        term = bdot(weights, zbuf[c, :, :N])
        if first:
            tot[r] = term
        else:
            tot[r] += term

    is_upper = [(leaf // 2**level) % 2 for level in range(LEVELS)]
    for level in range(LEVELS):
        index = mskel_ref[level]
        index = lax.rem(index + N * is_upper[level], 2 * N)
        wide = (iota((2 * N, N), 0) == index) & (column < ranks_ref[0, level + 1])
        onehots[level] = bdot(eye, wide.astype(F32).astype(BF16), NT).astype(BF16)

    def dead_rows(x, row0, rank):
        rows = x.shape[0]
        gone = iota((rows, AUG), 0) + row0 >= rank
        at = iota((rows, AUG), 1)
        x = jnp.where(gone & (at == 64), DEAD, x)
        return jnp.where(gone & (at == 67), 1.0, x).astype(BF16)

    def total_of(dst):
        total = dst[0].astype(F32)
        for d in range(1, RING):
            total += dst[d].astype(F32)
        return total

    seen = set()
    todo = [(OWN, OWN)]

    def work(pairs):
        for r, c in pairs:
            block(r, c, all((r, k) not in seen for k in range(RING)))
            seen.add((r, c))

    for s in range(1, 5):
        for part in range(2):
            for axis in range(2):
                for way in range(2):
                    copy = flying.pop((axis, way, s, part), None)
                    if copy is not None:
                        copy.wait_recv()
                        if s < 3 or (s == 3 and part == way):
                            if way == 0:
                                flying[axis, 0, s + 1, part] = right(axes[axis], s + 1, part)
                            else:
                                flying[axis, 1, s + 1, part] = left(axes[axis], s + 1, part)
            if s == 1 and part == 1:
                psp[...] = pick(hot, samples)
                picked_rs = scatter(psp, prz, zpeer, z, CUT)
            if s == 2 and part == 0:
                arrive(chosen_rs)
                total = csp[own_rows(z, CUT), :].astype(F32)
                for d in range(1, RING):
                    total += crz[d].astype(F32)
                cry[y] = total.astype(BF16)
                chosen_ag = spread(cry, ypeer, y)
            if s == 3 and part == 1:
                arrive(chosen_ag)
                cz[...] = dead_rows(total_of(cry), z * CUT, ranks_ref[0, 0])
                och[0, own_rows(z, CUT), :] = cz[...]
                chosen_all = gather(och.at[0], zpeer, z, CUT)
            cut = len(todo) // 2
            work(todo[:cut] if part == 0 else todo)
            todo = todo[cut:] if part == 0 else []
        known = range(max(0, OWN - s), OWN + s + 1)
        todo = [(r, c) for c in known for r in known if (r, c) not in seen]

    arrive(picked_rs)
    total = psp[own_rows(z, CUT), :]
    for d in range(1, RING):
        total += prz[d]
    for c in range(RING):
        weights = gauss(cz[...], zbuf[c, :, N:]).astype(BF16)
        total -= bdot(weights, zbuf[c, :, :N])
    pry[y] = total
    picked_ag = spread(pry, ypeer, y)
    work(todo)

    flows = []

    def sum_step(s):
        if s > 0:
            arrive(flows[-1])
            if s == 1:
                tot[OWN - 3, :hr] += rsb[0, 0, :hr]
                tot[OWN + 3, hr:] += rsb[1, 0, hr:]
            else:
                tot[OWN - 4 + s] += rsb[0, s - 1]
                tot[OWN + 4 - s] += rsb[1, s - 1]
        if s == 0:
            flows.append([
                send(tot.at[OWN + 4, top], rsb.at[0, 0, top], ypeer(1)),
                send(tot.at[OWN + 4, bottom], rsb.at[1, 0, bottom], ypeer(-1)),
            ])
        elif s < 4:
            flows.append([
                send(tot.at[OWN - 4 + s], rsb.at[0, s], ypeer(1)),
                send(tot.at[OWN + 4 - s], rsb.at[1, s], ypeer(-1)),
            ])

    sum_step(0)
    sh, sl = split2(samples)
    mt = bdot(omega_t, sh) + bdot(omega_t, sl)
    for r in range(RING):
        th, tl = split2(tot[r])
        turned = ybuf[r, :, :N]
        mt -= bdot(turned, th) + bdot(turned, tl)
    mtp[...] = mt
    halves = ((0, z, y, zpeer, ypeer), (hr, y, z, ypeer, zpeer))
    piece = hr // RING
    stage = []
    for i, (start, pos, other, first, second) in enumerate(halves):
        stage += scatter(mtp.at[pl.ds(start, hr)], mr1.at[i], first, pos, piece)

    arrive(picked_ag)
    opk[0, own_rows(z, CUT), :] = total_of(pry)
    picked_all = gather(opk.at[0], zpeer, z, CUT)

    arrive(stage)
    stage = []
    for i, (start, pos, other, first, second) in enumerate(halves):
        at = pl.ds(pl.multiple_of(start + pos * piece, piece), piece)
        total = mtp[at, :]
        for d in range(1, RING):
            total += mr1[i, d]
        mr2[i, other] = total
        stage += spread(mr2.at[i], second, other)
    arrive(stage)
    stage = []
    for i, (start, pos, other, first, second) in enumerate(halves):
        at = pl.ds(pl.multiple_of(start + pos * piece, piece), piece)
        mfull[at, :] = total_of(mr2.at[i])
        stage += gather(mfull, first, pos, piece, start)

    arrive(chosen_all)
    arrive(picked_all)

    core = leaf % 2
    mate = partners[0]
    mine = pl.ds(pl.multiple_of(core * hr, hr), hr)

    def offer(src, dst, level):
        if level == 0:
            return [send(src.at[0], dst.at[0], mate)]
        return [send(src.at[level, mine], dst.at[level, mine], partners[level])]

    def accept(group, dst, level):
        arrive(group)
        if level > 0:
            return [send(dst.at[level, mine], dst.at[level, mine], mate)]
        return []

    def swap(level):
        return [offer(och, xch, level), offer(opk, xpk, level)]

    early = swap(0)
    picked = opk[0]
    inverse = ridge_inverse(picked)
    turn_out[...] = dot3(inverse, picked)
    arrive(stage)
    ocm[0] = dot6(inverse, dot6(picked, mfull[...], NT))
    late = offer(ocm, xcm, 0)

    row = iota((AUG, AUG), 0)
    col = iota((AUG, AUG), 1)
    turn = jnp.where((row >= 64) & (row < 67), row + 3, jnp.where((row >= 67) & (row < 70), row - 3, row))
    turn = (turn == col).astype(F32).astype(BF16)

    for level in range(1, LEVELS + 1):
        last = level - 1
        handed = accept(early[0], xch, last) + accept(early[1], xpk, last)
        arrive(handed[:1])
        own_f, other_f = och[last], xch[last]
        own_g = bdot(own_f, turn).astype(BF16)
        other_g = bdot(other_f, turn).astype(BF16)
        coupling = gauss(own_f, other_g)
        coupling_t = gauss(other_f, own_g)
        coup_out[0, last] = coupling
        onehot = onehots[last]
        fresh = bdot(onehot[:, :N], own_f) + bdot(onehot[:, N:], other_f)
        och[level] = dead_rows(fresh, 0, ranks_ref[0, level])
        arrive(handed[1:])
        arrive(accept(late, xcm, last))
        co[:N] = ocm[last]
        co[N:] = xcm[last]
        cy[:N] = opk[last] - dot3(coupling, xcm[last])
        cy[N:] = xpk[last] - dot3(coupling_t, ocm[last])
        cand = cy[...]
        picked = pick(onehot, cand)
        opk[level] = picked
        if level < LEVELS:
            early = swap(level)
        sum_step(level)
        inverse = ridge_inverse(picked)
        weight = dot6(dot6(picked, cand, NT), co[...])
        compressed = dot6(inverse, weight)
        if level < LEVELS:
            ocm[level] = compressed
            late = offer(ocm, xcm, level)
        else:
            top_out[0] = compressed
        interp = dot3(cand, dot3(inverse, picked), NT)
        at = is_upper[last] * N
        node_out[0, last, pl.ds(pl.multiple_of(at, N), N), :] = interp[:N]
        node_out[0, last, pl.ds(pl.multiple_of(N - at, N), N), :] = interp[N:]

    sum_step(4)
    diag_out[...] = tot[OWN]
    for copy in copies:
        copy.wait_send()


def finish(samples_ref, diag_ref, turn_ref, node_ref, coup_ref, top_ref, leaf_out, node_out, coup_out, top_out, sems):
    moves = [
        pltpu.make_async_copy(src, dst, sems.at[i])
        for i, (src, dst) in enumerate(((node_ref, node_out), (coup_ref, coup_out), (top_ref, top_out)))
    ]
    for move in moves:
        move.start()
    leaf_out[...] = dot3(samples_ref[...] - diag_ref[...], turn_ref[...], NT)
    for move in moves:
        move.wait()


N_COPIES = 28 + 6 * (RING - 1) + 6 * (RING - 1) + 8 + 3 + 6 * (LEVELS - 1)


def shards(points, omega, samples, ranks, leaf_skeleton, merge_skeleton):
    vmem = pl.BlockSpec(memory_space=pltpu.VMEM)
    parts = pl.pallas_call(
        body,
        out_shape=(
            jax.ShapeDtypeStruct((N, N), F32),
            jax.ShapeDtypeStruct((N, N), F32),
            jax.ShapeDtypeStruct((1, LEVELS, 2 * N, N), F32),
            jax.ShapeDtypeStruct((1, LEVELS, N, N), F32),
            jax.ShapeDtypeStruct((1, N, N), F32),
        ),
        in_specs=[vmem] * 5 + [pl.BlockSpec(memory_space=pltpu.SMEM)],
        out_specs=(vmem,) * 5,
        scratch_shapes=[
            pltpu.VMEM((RING, N, N + AUG), BF16),
            pltpu.VMEM((RING, N, N + AUG), BF16),
            pltpu.VMEM((RING, N, N), F32),
            pltpu.VMEM((2, 4, N, N), F32),
            pltpu.VMEM((N, AUG), BF16),
            pltpu.VMEM((RING, CUT, AUG), BF16),
            pltpu.VMEM((RING, CUT, AUG), BF16),
            pltpu.VMEM((CUT, AUG), BF16),
            pltpu.VMEM((LEVELS + 1, N, AUG), BF16),
            pltpu.VMEM((LEVELS, N, AUG), BF16),
            pltpu.VMEM((N, N), F32),
            pltpu.VMEM((RING, CUT, N), F32),
            pltpu.VMEM((RING, CUT, N), F32),
            pltpu.VMEM((LEVELS + 1, N, N), F32),
            pltpu.VMEM((LEVELS, N, N), F32),
            pltpu.VMEM((N, N), F32),
            pltpu.VMEM((2, RING, CUT // 2, N), F32),
            pltpu.VMEM((2, RING, CUT // 2, N), F32),
            pltpu.VMEM((N, N), F32),
            pltpu.VMEM((LEVELS, N, N), F32),
            pltpu.VMEM((LEVELS, N, N), F32),
            pltpu.VMEM((LEVELS, N, 2 * N), BF16),
            pltpu.VMEM((2 * N, N), F32),
            pltpu.VMEM((2 * N, N), F32),
            pltpu.SemaphoreType.DMA((N_COPIES,)),
            pltpu.SemaphoreType.DMA((N_COPIES,)),
        ],
        compiler_params=pltpu.CompilerParams(
            collective_id=0, has_side_effects=True, vmem_limit_bytes=40 * 2**20
        ),
    )(omega, points.T, samples, leaf_skeleton, merge_skeleton.transpose(1, 0, 2), ranks)
    hold = pl.BlockSpec(memory_space=pl.ANY)
    return pl.pallas_call(
        finish,
        out_shape=(jax.ShapeDtypeStruct((N, N), F32),)
        + tuple(jax.ShapeDtypeStruct(part.shape, F32) for part in parts[2:]),
        in_specs=[vmem] * 3 + [hold] * 3,
        out_specs=(vmem,) + (hold,) * 3,
        scratch_shapes=[pltpu.SemaphoreType.DMA((3,))],
        compiler_params=pltpu.CompilerParams(vmem_limit_bytes=16 * 2**20),
    )(samples, *parts)


def solution(mesh):
    in_specs = (
        P(("leaf", "sub"), None),
        P(("leaf", "sub"), None),
        P(("leaf", "sub"), None),
        P("leaf", None),
        P("leaf", None),
        P("leaf", None, None),
    )
    out_specs = (
        P(("leaf", "sub"), None),
        P("leaf", None, None, None),
        P("leaf", None, None, None),
        P("leaf", None, None),
    )
    return jax.shard_map(shards, mesh=mesh, in_specs=in_specs, out_specs=out_specs, check_vma=False)
```

time: 135 us -> 123 us (0.911)
  Pallas kernels: 125 us -> 117 us
  local copies, waits for them, and re-layouts: 8.77 us -> 4.62 us
    pallas_call x1, Pallas kernels: 125 us -> 115 us  [shards(): pl.pallas_call(body, out_shape=(jax.ShapeDtypeStruct((N, N), F32), jax.Sh...]
    unnamed x10 -> x12, local copies, waits for them, and re-layouts: 8.77 us -> 4.62 us
    pallas_call x0 -> x1, Pallas kernels: none -> 2.23 us  [shards(): pl.pallas_call(finish, out_shape=(jax.ShapeDtypeStruct((N, N), F32),) + t...]
where the time goes in v2:
time: 123 us
  Pallas kernels  117 us (95%)
  local copies, waits for them, and re-layouts  4.62 us (4%)
    pallas_call x1, Pallas kernels, shards(): pl.pallas_call(body, out_shape=(jax.ShapeDtypeStruct((N, N), F32), jax.Sh...  115 us
    unnamed x12, local copies, waits for them, and re-layouts  4.62 us

profile of v2, /device:TPU:1, one launch (start us, length us, event | category | flops | bytes accessed | tf_op | source)
XLA Modules:
  0.0 122.5 jit_solution(17971253860036844168)
XLA Ops:
  0.6 0.0 copy-start
  0.6 0.9 copy-done
  1.6 0.0 copy-start.1
  1.6 0.9 copy-done.1
  2.5 0.0 copy-start.2
  2.5 0.8 copy-done.2
  3.2 0.0 copy-start.3
  3.2 0.7 copy-done.3
  3.9 0.0 copy-start.4
  3.9 0.7 copy-done.4
  4.6 0.0 copy-start.5
  4.6 0.7 copy-done.5
  5.3 114.8 %shard_map.93 = (f32[256,256]{1,0:T(8,128)S(1)}, f32[256,256]{1,0:T(8,128)S(1)}, f32[1,3,512,256]{3,2,1,0:T(8,128)S(1)}, f32[1,3,256,256]{3,2,1,0:T(8,128)S(1)}, f32[1,256,256]{2,1,0:T(8,128)S(1)}) custom-call(bf16[256,256]{1,0:T(8,128)(2,1)S(1)} %copy-done.1, bf16[64,256]{1,0:T(8,128)(2,1)S(1)} %bitcast.2, f32[256,256]{1,0:T(8,128)S(1)} %copy-done, ...), custom_call_target="tpu_custom_call" | custom-call | tf_op jit(solution)/shard_map/pallas_call | solution.py:447
  120.1 2.2 %shard_map.94 = (f32[256,256]{1,0:T(8,128)}, f32[1,3,512,256]{3,2,1,0:T(8,128)}, f32[1,3,256,256]{3,2,1,0:T(8,128)}, f32[1,256,256]{2,1,0:T(8,128)}) custom-call(f32[256,256]{1,0:T(8,128)S(1)} %copy-done, f32[256,256]{1,0:T(8,128)S(1)} %get-tuple-element.9.diag_ref, f32[256,256]{1,0:T(8,128)S(1)} %get-tuple-element.10.turn_ref, ...), custom_call_target="tpu_custom_call" | custom-call | tf_op jit(solution)/shard_map/pallas_call | solution.py:491
Async XLA Ops:
  0.6 1.0 copy-start
  1.6 0.9 copy-start.1
  2.5 0.8 copy-start.2
  3.2 0.7 copy-start.3
  3.9 0.7 copy-start.4
  4.6 0.7 copy-start.5

commit v3 on v2

--- a/solution.py
+++ b/solution.py
@@ -11,6 +11,7 @@
 N = 256
 AUG = 128
 CUT = N // RING
+PIECES = 4
 LEVELS = 3
 OWN = RING // 2 - 1
 NN = ((1,), (0,))
@@ -68,21 +69,31 @@
     return lax.broadcasted_iota(jnp.int32, shape, dim)
 
 
-def ridge_inverse(p):
+def ridge_factor(p):
     gram = dot6(p, p, NT)
     inv_shift = 1.0 / (jnp.sum(p * p) / N + 1e-06)
     eye = (iota((N, N), 0) == iota((N, N), 1)).astype(F32)
     b = gram * inv_shift + eye
     x = ALPHA * eye - BETA * b
     e = eye - dot3(b, x)
-    for w in RATES:
-        eh, el = split2(e)
-        xh, xl = split2(x)
-        e2 = bdot(eh, eh) + (bdot(eh, el) + bdot(el, eh))
-        x = w * (x + (bdot(xh, eh) + (bdot(xh, el) + bdot(xl, eh))))
+    for step, w in enumerate(RATES):
+        if step < 4:
+            eh, el = split2(e)
+            xh, xl = split2(x)
+            e2 = bdot(eh, eh) + (bdot(eh, el) + bdot(el, eh))
+            x = w * (x + (bdot(xh, eh) + (bdot(xh, el) + bdot(xl, eh))))
+        else:
+            eh = e.astype(BF16)
+            e2 = bdot(eh, eh)
+            x = w * (x + bdot(x.astype(BF16), eh))
         e = (1.0 - w) * eye + w * e2
-    x = x + dot6(x, eye - dot6(b, x))
-    return x * inv_shift
+    return b, x, inv_shift
+
+
+def ridge_solve(factor, right):
+    b, x, inv_shift = factor
+    first = dot3(x, right)
+    return (first + dot3(x, right - dot6(b, first))) * inv_shift
 
 
 def gauss(left_f, right_g):
@@ -90,14 +101,30 @@
 
 
 def body(
-    omega_ref, points_ref, samples_ref, skel_ref, mskel_ref, ranks_ref,
-    diag_out, turn_out, node_out, coup_out, top_out,
+    omega_hbm, points_hbm, samples_hbm, skel_hbm, mskel_hbm, ranks_hbm,
+    diag_hbm, turn_hbm, node_hbm, coup_hbm, top_hbm,
     zbuf, ybuf, tot, rsb,
     csp, crz, cry, cz, och, xch,
     psp, prz, pry, opk, xpk,
     mtp, mr1, mr2, mfull, ocm, xcm, onehots, cy, co,
-    send_sem, recv_sem,
+    points_ref, omega_ref, skel_ref, ranks_ref, samples_ref, mskel_ref, load_sem,
+    turn_out, node_out, coup_out, top_out, store_sem, send_sem, recv_sem,
 ):
+    loads = [
+        pltpu.make_async_copy(src, dst, load_sem.at[i])
+        for i, (src, dst) in enumerate((
+            (points_hbm, points_ref), (omega_hbm, omega_ref), (skel_hbm, skel_ref),
+            (ranks_hbm, ranks_ref), (samples_hbm, samples_ref), (mskel_hbm, mskel_ref),
+        ))
+    ]
+    for load in loads:
+        load.start()
+    stores = []
+
+    def store(src, dst):
+        stores.append(pltpu.make_async_copy(src, dst, store_sem.at[len(stores)]))
+        stores[-1].start()
+
     sub = lax.axis_index("sub")
     leaf = lax.axis_index("leaf")
     z = sub // RING
@@ -135,6 +162,9 @@
         for copy in group:
             copy.wait_recv()
 
+    for load in loads[:4]:
+        load.wait()
+
     eye = (iota((N, N), 0) == iota((N, N), 1)).astype(BF16)
     padded = jnp.concatenate([points_ref[...], jnp.zeros((AUG - 64, N), BF16)], axis=0)
     plain = bdot(eye, padded, NT)
@@ -150,19 +180,11 @@
 
     feat = place(64, 67)
     omega = omega_ref[...]
-    samples = samples_ref[...]
     omega_t = bdot(eye, omega, NT).astype(BF16)
     zbuf[OWN, :, :N] = omega
     zbuf[OWN, :, N:] = place(67, 64)
     ybuf[OWN, :, :N] = omega_t
     ybuf[OWN, :, N:] = feat
-    column = iota((1, N), 1)
-    offset = skel_ref[...] - sub * N
-    hits = (iota((N, N), 0) == offset) & (column < ranks_ref[0, 0])
-    hits = hits.astype(F32).astype(BF16)
-    hot = bdot(eye, hits, NT).astype(BF16)
-    csp[...] = bdot(hot, feat).astype(BF16)
-
     pl.semaphore_wait(barrier, 2 * (RING - 1) + LEVELS)
 
     def scatter(src, dst, peer, pos, rows):
@@ -184,34 +206,39 @@
         at = pl.ds(pl.multiple_of(start + pos * rows, rows), rows)
         return [send(full.at[at], full.at[at], peer(d)) for d in range(1, RING)]
 
-    chosen_rs = scatter(csp, crz, zpeer, z, CUT)
-
     hr = N // 2
     top, bottom = pl.ds(0, hr), pl.ds(hr, hr)
 
     def right(axis, s, part):
         buf, peer = axis
-        at = top if part == 0 else bottom
+        at = pl.ds(part * (N // PIECES), N // PIECES)
         return send(buf.at[OWN + s - 1, at], buf.at[OWN + s, at], peer(1))
 
     def left(axis, s, part):
         buf, peer = axis
-        at = top if part == 0 else bottom
+        at = pl.ds(part * (N // PIECES), N // PIECES)
         to = OWN - s if s < 4 else OWN + 4
         return send(buf.at[OWN - s + 1, at], buf.at[to, at], peer(-1))
 
     axes = ((zbuf, zpeer), (ybuf, ypeer))
+    ways = (right, left)
     flying = {}
 
-    def launch(axis, s, part):
-        if s < 4 or part == 0:
-            flying[axis, 0, s, part] = right(axes[axis], s, part)
-        if s < 4 or part == 1:
-            flying[axis, 1, s, part] = left(axes[axis], s, part)
-
-    for part in range(2):
+    def launch(axis, way, s, part):
+        if s < 4 or part * 2 // PIECES == way:
+            flying[axis, way, s, part] = ways[way](axes[axis], s, part)
+
+    for part in range(PIECES):
         for axis in range(2):
-            launch(axis, 1, part)
+            for way in range(2):
+                launch(axis, way, 1, part)
+
+    column = iota((1, N), 1)
+    offset = skel_ref[...] - sub * N
+    hits = (iota((N, N), 0) == offset) & (column < ranks_ref[0, 0])
+    hot = bdot(eye, hits.astype(F32).astype(BF16), NT).astype(BF16)
+    csp[...] = bdot(hot, feat).astype(BF16)
+    chosen_rs = scatter(csp, crz, zpeer, z, CUT)
 
     def block(r, c, first):
         weights = gauss(ybuf[r, :, N:], zbuf[c, :, N:]).astype(BF16)
@@ -221,6 +248,7 @@
         else:
             tot[r] += term
 
+    loads[5].wait()
     is_upper = [(leaf // 2**level) % 2 for level in range(LEVELS)]
     for level in range(LEVELS):
         index = mskel_ref[level]
@@ -250,19 +278,17 @@
             seen.add((r, c))
 
     for s in range(1, 5):
-        for part in range(2):
+        for part in range(PIECES):
             for axis in range(2):
                 for way in range(2):
                     copy = flying.pop((axis, way, s, part), None)
                     if copy is not None:
                         copy.wait_recv()
-                        if s < 3 or (s == 3 and part == way):
-                            if way == 0:
-                                flying[axis, 0, s + 1, part] = right(axes[axis], s + 1, part)
-                            else:
-                                flying[axis, 1, s + 1, part] = left(axes[axis], s + 1, part)
-            if s == 1 and part == 1:
-                psp[...] = pick(hot, samples)
+                        if s < 4:
+                            launch(axis, way, s + 1, part)
+            if s == 1 and part == PIECES - 1:
+                loads[4].wait()
+                psp[...] = pick(hot, samples_ref[...])
                 picked_rs = scatter(psp, prz, zpeer, z, CUT)
             if s == 2 and part == 0:
                 arrive(chosen_rs)
@@ -271,14 +297,14 @@
                     total += crz[d].astype(F32)
                 cry[y] = total.astype(BF16)
                 chosen_ag = spread(cry, ypeer, y)
-            if s == 3 and part == 1:
+            if s == 3 and part == PIECES - 1:
                 arrive(chosen_ag)
                 cz[...] = dead_rows(total_of(cry), z * CUT, ranks_ref[0, 0])
                 och[0, own_rows(z, CUT), :] = cz[...]
                 chosen_all = gather(och.at[0], zpeer, z, CUT)
-            cut = len(todo) // 2
-            work(todo[:cut] if part == 0 else todo)
-            todo = todo[cut:] if part == 0 else []
+            cut = len(todo) // (PIECES - part)
+            work(todo[:cut])
+            todo = todo[cut:]
         known = range(max(0, OWN - s), OWN + s + 1)
         todo = [(r, c) for c in known for r in known if (r, c) not in seen]
 
@@ -316,7 +342,7 @@
             ])
 
     sum_step(0)
-    sh, sl = split2(samples)
+    sh, sl = split2(samples_ref[...])
     mt = bdot(omega_t, sh) + bdot(omega_t, sl)
     for r in range(RING):
         th, tl = split2(tot[r])
@@ -372,11 +398,12 @@
 
     early = swap(0)
     picked = opk[0]
-    inverse = ridge_inverse(picked)
-    turn_out[...] = dot3(inverse, picked)
+    factor = ridge_factor(picked)
     arrive(stage)
-    ocm[0] = dot6(inverse, dot6(picked, mfull[...], NT))
+    ocm[0] = ridge_solve(factor, dot6(picked, mfull[...], NT))
     late = offer(ocm, xcm, 0)
+    turn_out[...] = ridge_solve(factor, picked)
+    store(turn_out, turn_hbm)
 
     row = iota((AUG, AUG), 0)
     col = iota((AUG, AUG), 1)
@@ -392,7 +419,8 @@
         other_g = bdot(other_f, turn).astype(BF16)
         coupling = gauss(own_f, other_g)
         coupling_t = gauss(other_f, own_g)
-        coup_out[0, last] = coupling
+        coup_out[last] = coupling
+        store(coup_out.at[last], coup_hbm.at[0, last])
         onehot = onehots[last]
         fresh = bdot(onehot[:, :N], own_f) + bdot(onehot[:, N:], other_f)
         och[level] = dead_rows(fresh, 0, ranks_ref[0, level])
@@ -408,21 +436,25 @@
         if level < LEVELS:
             early = swap(level)
         sum_step(level)
-        inverse = ridge_inverse(picked)
+        factor = ridge_factor(picked)
         weight = dot6(dot6(picked, cand, NT), co[...])
-        compressed = dot6(inverse, weight)
+        compressed = ridge_solve(factor, weight)
         if level < LEVELS:
             ocm[level] = compressed
             late = offer(ocm, xcm, level)
         else:
-            top_out[0] = compressed
-        interp = dot3(cand, dot3(inverse, picked), NT)
+            top_out[...] = compressed
+            store(top_out, top_hbm.at[0])
+        interp = dot3(cand, ridge_solve(factor, picked), NT)
         at = is_upper[last] * N
-        node_out[0, last, pl.ds(pl.multiple_of(at, N), N), :] = interp[:N]
-        node_out[0, last, pl.ds(pl.multiple_of(N - at, N), N), :] = interp[N:]
+        node_out[last, pl.ds(pl.multiple_of(at, N), N), :] = interp[:N]
+        node_out[last, pl.ds(pl.multiple_of(N - at, N), N), :] = interp[N:]
+        store(node_out.at[last], node_hbm.at[0, last])
 
     sum_step(4)
-    diag_out[...] = tot[OWN]
+    store(tot.at[OWN], diag_hbm)
+    for move in stores:
+        move.wait()
     for copy in copies:
         copy.wait_send()
 
@@ -439,7 +471,7 @@
         move.wait()
 
 
-N_COPIES = 28 + 6 * (RING - 1) + 6 * (RING - 1) + 8 + 3 + 6 * (LEVELS - 1)
+N_COPIES = 14 * PIECES + 6 * (RING - 1) + 6 * (RING - 1) + 8 + 3 + 6 * (LEVELS - 1)
 
 
 def shards(points, omega, samples, ranks, leaf_skeleton, merge_skeleton):
@@ -453,8 +485,8 @@
             jax.ShapeDtypeStruct((1, LEVELS, N, N), F32),
             jax.ShapeDtypeStruct((1, N, N), F32),
         ),
-        in_specs=[vmem] * 5 + [pl.BlockSpec(memory_space=pltpu.SMEM)],
-        out_specs=(vmem,) * 5,
+        in_specs=[pl.BlockSpec(memory_space=pltpu.HBM)] * 6,
+        out_specs=(pl.BlockSpec(memory_space=pltpu.HBM),) * 5,
         scratch_shapes=[
             pltpu.VMEM((RING, N, N + AUG), BF16),
             pltpu.VMEM((RING, N, N + AUG), BF16),
@@ -480,11 +512,23 @@
             pltpu.VMEM((LEVELS, N, 2 * N), BF16),
             pltpu.VMEM((2 * N, N), F32),
             pltpu.VMEM((2 * N, N), F32),
+            pltpu.VMEM(points.shape[::-1], BF16),
+            pltpu.VMEM(omega.shape, BF16),
+            pltpu.VMEM(leaf_skeleton.shape, jnp.int32),
+            pltpu.SMEM(ranks.shape, jnp.int32),
+            pltpu.VMEM(samples.shape, F32),
+            pltpu.VMEM((LEVELS, 1, N), jnp.int32),
+            pltpu.SemaphoreType.DMA((6,)),
+            pltpu.VMEM((N, N), F32),
+            pltpu.VMEM((LEVELS, 2 * N, N), F32),
+            pltpu.VMEM((LEVELS, N, N), F32),
+            pltpu.VMEM((N, N), F32),
+            pltpu.SemaphoreType.DMA((2 * LEVELS + 3,)),
             pltpu.SemaphoreType.DMA((N_COPIES,)),
             pltpu.SemaphoreType.DMA((N_COPIES,)),
         ],
         compiler_params=pltpu.CompilerParams(
-            collective_id=0, has_side_effects=True, vmem_limit_bytes=40 * 2**20
+            collective_id=0, has_side_effects=True, vmem_limit_bytes=54 * 2**20
         ),
     )(omega, points.T, samples, leaf_skeleton, merge_skeleton.transpose(1, 0, 2), ranks)
     hold = pl.BlockSpec(memory_space=pl.ANY)
@@ -495,7 +539,7 @@
         in_specs=[vmem] * 3 + [hold] * 3,
         out_specs=(vmem,) + (hold,) * 3,
         scratch_shapes=[pltpu.SemaphoreType.DMA((3,))],
-        compiler_params=pltpu.CompilerParams(vmem_limit_bytes=16 * 2**20),
+        compiler_params=pltpu.CompilerParams(vmem_limit_bytes=54 * 2**20),
     )(samples, *parts)
 
 

time: 123 us -> 199 us (1.62)
  Pallas kernels: 117 us -> 198 us
  local copies, waits for them, and re-layouts: 4.62 us -> 0 us
    pallas_call x1, Pallas kernels: 2.23 us -> 82.3 us  [shards(): pl.pallas_call(finish, out_shape=(jax.ShapeDtypeStruct((N, N), F32),) + t...]
    unnamed x12 -> x0, local copies, waits for them, and re-layouts: 4.62 us -> none
where the time goes in v3:
time: 199 us
  Pallas kernels  198 us (99%)
    pallas_call x1, Pallas kernels, shards(): pl.pallas_call(body, out_shape=(jax.ShapeDtypeStruct((N, N), F32), jax.Sh...  116 us
    pallas_call x1, Pallas kernels, shards(): pl.pallas_call(finish, out_shape=(jax.ShapeDtypeStruct((N, N), F32),) + t...  82.3 us

profile of v3, /device:TPU:1, one launch (start us, length us, event | category | flops | bytes accessed | tf_op | source)
XLA Modules:
  0.0 198.8 jit_solution(5321582170495033783)
XLA Ops:
  0.6 115.6 %shard_map.93 = (f32[256,256]{1,0:T(8,128)}, f32[256,256]{1,0:T(8,128)}, f32[1,3,512,256]{3,2,1,0:T(8,128)}, f32[1,3,256,256]{3,2,1,0:T(8,128)}, f32[1,256,256]{2,1,0:T(8,128)}) custom-call(bf16[256,256]{1,0:T(8,128)(2,1)} %omega_hbm.1, bf16[64,256]{1,0:T(8,128)(2,1)} %bitcast.2, f32[256,256]{1,0:T(8,128)} %samples_ref.1, s32[1,256]{1,0:T(1,128)} %skel_hbm.1, ...), custom_call_target="tpu_custom_call" | custom-call | tf_op jit(solution)/shard_map/pallas_call | solution.py:479
  116.3 82.3 %shard_map.94 = (f32[256,256]{1,0:T(8,128)}, f32[1,3,512,256]{3,2,1,0:T(8,128)}, f32[1,3,256,256]{3,2,1,0:T(8,128)}, f32[1,256,256]{2,1,0:T(8,128)}) custom-call(f32[256,256]{1,0:T(8,128)} %samples_ref.1, f32[256,256]{1,0:T(8,128)} %get-tuple-element.9.diag_ref, f32[256,256]{1,0:T(8,128)} %get-tuple-element.10.turn_ref, ...), custom_call_target="tpu_custom_call" | custom-call | tf_op jit(solution)/shard_map/pallas_call | solution.py:535

commit v4 on v3

--- a/solution.py
+++ b/solution.py
@@ -106,7 +106,7 @@
     zbuf, ybuf, tot, rsb,
     csp, crz, cry, cz, och, xch,
     psp, prz, pry, opk, xpk,
-    mtp, mr1, mr2, mfull, ocm, xcm, onehots, cy, co,
+    kept, mtp, mr1, mr2, mfull, ocm, xcm, onehots, cy, co,
     points_ref, omega_ref, skel_ref, ranks_ref, samples_ref, mskel_ref, load_sem,
     turn_out, node_out, coup_out, top_out, store_sem, send_sem, recv_sem,
 ):
@@ -277,16 +277,15 @@
             block(r, c, all((r, k) not in seen for k in range(RING)))
             seen.add((r, c))
 
-    for s in range(1, 5):
+    for s in range(1, 4):
         for part in range(PIECES):
             for axis in range(2):
                 for way in range(2):
                     copy = flying.pop((axis, way, s, part), None)
                     if copy is not None:
                         copy.wait_recv()
-                        if s < 4:
-                            launch(axis, way, s + 1, part)
-            if s == 1 and part == PIECES - 1:
+                        launch(axis, way, s + 1, part)
+            if s == 2 and part == PIECES - 1:
                 loads[4].wait()
                 psp[...] = pick(hot, samples_ref[...])
                 picked_rs = scatter(psp, prz, zpeer, z, CUT)
@@ -308,6 +307,34 @@
         known = range(max(0, OWN - s), OWN + s + 1)
         todo = [(r, c) for c in known for r in known if (r, c) not in seen]
 
+    work(todo)
+    sh, sl = split2(samples_ref[...])
+    mt = bdot(omega_t, sh) + bdot(omega_t, sl)
+    far = RING - 1
+    for r in range(far):
+        th, tl = split2(tot[r])
+        turned = ybuf[r, :, :N]
+        mt -= bdot(turned, th) + bdot(turned, tl)
+    mtp[...] = mt
+    for copy in flying.values():
+        copy.wait_recv()
+    for c in range(far):
+        block(far, c, c == 0)
+    columns = jnp.zeros((N, N), F32)
+    for r in range(RING):
+        weights = gauss(ybuf[r, :, N:], zbuf[far, :, N:]).astype(BF16)
+        kept[r] = weights
+        columns += bdot(ybuf[r, :, :N], weights)
+    th, tl = split2(tot[far])
+    vh, vl = split2(columns)
+    turned, plain_omega = ybuf[far, :, :N], zbuf[far, :, :N]
+    mtp[...] -= bdot(turned, th) + bdot(turned, tl) + bdot(vh, plain_omega) + bdot(vl, plain_omega)
+    halves = ((0, z, y, zpeer, ypeer), (hr, y, z, ypeer, zpeer))
+    piece = hr // RING
+    stage = []
+    for i, (start, pos, other, first, second) in enumerate(halves):
+        stage += scatter(mtp.at[pl.ds(start, hr)], mr1.at[i], first, pos, piece)
+
     arrive(picked_rs)
     total = psp[own_rows(z, CUT), :]
     for d in range(1, RING):
@@ -317,7 +344,8 @@
         total -= bdot(weights, zbuf[c, :, :N])
     pry[y] = total
     picked_ag = spread(pry, ypeer, y)
-    work(todo)
+    for r in range(RING):
+        tot[r] += bdot(kept[r], zbuf[far, :, :N])
 
     flows = []
 
@@ -341,24 +369,6 @@
                 send(tot.at[OWN + 4 - s], rsb.at[1, s], ypeer(-1)),
             ])
 
-    sum_step(0)
-    sh, sl = split2(samples_ref[...])
-    mt = bdot(omega_t, sh) + bdot(omega_t, sl)
-    for r in range(RING):
-        th, tl = split2(tot[r])
-        turned = ybuf[r, :, :N]
-        mt -= bdot(turned, th) + bdot(turned, tl)
-    mtp[...] = mt
-    halves = ((0, z, y, zpeer, ypeer), (hr, y, z, ypeer, zpeer))
-    piece = hr // RING
-    stage = []
-    for i, (start, pos, other, first, second) in enumerate(halves):
-        stage += scatter(mtp.at[pl.ds(start, hr)], mr1.at[i], first, pos, piece)
-
-    arrive(picked_ag)
-    opk[0, own_rows(z, CUT), :] = total_of(pry)
-    picked_all = gather(opk.at[0], zpeer, z, CUT)
-
     arrive(stage)
     stage = []
     for i, (start, pos, other, first, second) in enumerate(halves):
@@ -368,6 +378,10 @@
             total += mr1[i, d]
         mr2[i, other] = total
         stage += spread(mr2.at[i], second, other)
+    arrive(picked_ag)
+    opk[0, own_rows(z, CUT), :] = total_of(pry)
+    picked_all = gather(opk.at[0], zpeer, z, CUT)
+
     arrive(stage)
     stage = []
     for i, (start, pos, other, first, second) in enumerate(halves):
@@ -397,13 +411,13 @@
         return [offer(och, xch, level), offer(opk, xpk, level)]
 
     early = swap(0)
+    sum_step(0)
     picked = opk[0]
     factor = ridge_factor(picked)
     arrive(stage)
     ocm[0] = ridge_solve(factor, dot6(picked, mfull[...], NT))
     late = offer(ocm, xcm, 0)
-    turn_out[...] = ridge_solve(factor, picked)
-    store(turn_out, turn_hbm)
+    leaf_factor = factor
 
     row = iota((AUG, AUG), 0)
     col = iota((AUG, AUG), 1)
@@ -438,14 +452,19 @@
         sum_step(level)
         factor = ridge_factor(picked)
         weight = dot6(dot6(picked, cand, NT), co[...])
-        compressed = ridge_solve(factor, weight)
         if level < LEVELS:
-            ocm[level] = compressed
+            ocm[level] = ridge_solve(factor, weight)
             late = offer(ocm, xcm, level)
+            turned = ridge_solve(factor, picked)
         else:
-            top_out[...] = compressed
+            both = ridge_solve(factor, jnp.concatenate([weight, picked], axis=1))
+            top_out[...] = both[:, :N]
             store(top_out, top_hbm.at[0])
-        interp = dot3(cand, ridge_solve(factor, picked), NT)
+            turned = both[:, N:]
+        if level == 1:
+            turn_out[...] = ridge_solve(leaf_factor, opk[0])
+            store(turn_out, turn_hbm)
+        interp = dot3(cand, turned, NT)
         at = is_upper[last] * N
         node_out[last, pl.ds(pl.multiple_of(at, N), N), :] = interp[:N]
         node_out[last, pl.ds(pl.multiple_of(N - at, N), N), :] = interp[N:]
@@ -459,23 +478,37 @@
         copy.wait_send()
 
 
-def finish(samples_ref, diag_ref, turn_ref, node_ref, coup_ref, top_ref, leaf_out, node_out, coup_out, top_out, sems):
-    moves = [
-        pltpu.make_async_copy(src, dst, sems.at[i])
-        for i, (src, dst) in enumerate(((node_ref, node_out), (coup_ref, coup_out), (top_ref, top_out)))
-    ]
-    for move in moves:
-        move.start()
-    leaf_out[...] = dot3(samples_ref[...] - diag_ref[...], turn_ref[...], NT)
-    for move in moves:
-        move.wait()
+def finish(
+    samples_hbm, diag_hbm, turn_hbm, node_hbm, coup_hbm, top_hbm,
+    leaf_out, node_out, coup_out, top_out,
+    samples, diag, turn, leaf, node, coup, top, in_sem, out_sem,
+):
+    pairs = [(samples_hbm, samples), (diag_hbm, diag), (turn_hbm, turn)]
+    moves = [(top_hbm.at[0], top, top_out.at[0])]
+    for level in range(LEVELS):
+        moves.append((coup_hbm.at[0, level], coup.at[level], coup_out.at[0, level]))
+        moves.append((node_hbm.at[0, level], node.at[level], node_out.at[0, level]))
+    pairs += [move[:2] for move in moves]
+    loads = [pltpu.make_async_copy(*pair, in_sem.at[i]) for i, pair in enumerate(pairs)]
+    for load in loads:
+        load.start()
+    stores = [pltpu.make_async_copy(*move[1:], out_sem.at[i]) for i, move in enumerate(moves)]
+    for load in loads[:3]:
+        load.wait()
+    leaf[...] = dot3(samples[...] - diag[...], turn[...], NT)
+    stores.append(pltpu.make_async_copy(leaf, leaf_out, out_sem.at[len(moves)]))
+    stores[-1].start()
+    for load, store in zip(loads[3:], stores):
+        load.wait()
+        store.start()
+    for store in stores:
+        store.wait()
 
 
 N_COPIES = 14 * PIECES + 6 * (RING - 1) + 6 * (RING - 1) + 8 + 3 + 6 * (LEVELS - 1)
 
 
 def shards(points, omega, samples, ranks, leaf_skeleton, merge_skeleton):
-    vmem = pl.BlockSpec(memory_space=pltpu.VMEM)
     parts = pl.pallas_call(
         body,
         out_shape=(
@@ -503,6 +536,7 @@
             pltpu.VMEM((RING, CUT, N), F32),
             pltpu.VMEM((LEVELS + 1, N, N), F32),
             pltpu.VMEM((LEVELS, N, N), F32),
+            pltpu.VMEM((RING, N, N), BF16),
             pltpu.VMEM((N, N), F32),
             pltpu.VMEM((2, RING, CUT // 2, N), F32),
             pltpu.VMEM((2, RING, CUT // 2, N), F32),
@@ -536,9 +570,16 @@
         finish,
         out_shape=(jax.ShapeDtypeStruct((N, N), F32),)
         + tuple(jax.ShapeDtypeStruct(part.shape, F32) for part in parts[2:]),
-        in_specs=[vmem] * 3 + [hold] * 3,
-        out_specs=(vmem,) + (hold,) * 3,
-        scratch_shapes=[pltpu.SemaphoreType.DMA((3,))],
+        in_specs=[hold] * 6,
+        out_specs=(hold,) * 4,
+        scratch_shapes=[pltpu.VMEM((N, N), F32)] * 4
+        + [
+            pltpu.VMEM((LEVELS, 2 * N, N), F32),
+            pltpu.VMEM((LEVELS, N, N), F32),
+            pltpu.VMEM((N, N), F32),
+            pltpu.SemaphoreType.DMA((2 * LEVELS + 4,)),
+            pltpu.SemaphoreType.DMA((2 * LEVELS + 2,)),
+        ],
         compiler_params=pltpu.CompilerParams(vmem_limit_bytes=54 * 2**20),
     )(samples, *parts)
 

time: 199 us -> 117 us (0.59)
  Pallas kernels: 198 us -> 116 us
    pallas_call x1, Pallas kernels: 82.3 us -> 3.15 us  [shards(): pl.pallas_call(finish, out_shape=(jax.ShapeDtypeStruct((N, N), F32),) + t...]
    pallas_call x1, Pallas kernels: 116 us -> 113 us  [shards(): pl.pallas_call(body, out_shape=(jax.ShapeDtypeStruct((N, N), F32), jax.Sh...]
where the time goes in v4:
time: 117 us
  Pallas kernels  116 us (99%)
    pallas_call x1, Pallas kernels, shards(): pl.pallas_call(body, out_shape=(jax.ShapeDtypeStruct((N, N), F32), jax.Sh...  113 us
    pallas_call x1, Pallas kernels, shards(): pl.pallas_call(finish, out_shape=(jax.ShapeDtypeStruct((N, N), F32),) + t...  3.15 us

profile of v4, /device:TPU:1, one launch (start us, length us, event | category | flops | bytes accessed | tf_op | source)
XLA Modules:
  0.0 116.5 jit_solution(18061993409623434182)
XLA Ops:
  0.6 112.6 %shard_map.93 = (f32[256,256]{1,0:T(8,128)}, f32[256,256]{1,0:T(8,128)}, f32[1,3,512,256]{3,2,1,0:T(8,128)}, f32[1,3,256,256]{3,2,1,0:T(8,128)}, f32[1,256,256]{2,1,0:T(8,128)}) custom-call(bf16[256,256]{1,0:T(8,128)(2,1)} %omega_hbm.1, bf16[64,256]{1,0:T(8,128)(2,1)} %bitcast.2, f32[256,256]{1,0:T(8,128)} %samples_hbm.3, s32[1,256]{1,0:T(1,128)} %skel_hbm.1, ...), custom_call_target="tpu_custom_call" | custom-call | tf_op jit(solution)/shard_map/pallas_call | solution.py:512
  113.2 3.2 %shard_map.94 = (f32[256,256]{1,0:T(8,128)}, f32[1,3,512,256]{3,2,1,0:T(8,128)}, f32[1,3,256,256]{3,2,1,0:T(8,128)}, f32[1,256,256]{2,1,0:T(8,128)}) custom-call(f32[256,256]{1,0:T(8,128)} %samples_hbm.3, f32[256,256]{1,0:T(8,128)} %get-tuple-element.9.diag_hbm, f32[256,256]{1,0:T(8,128)} %get-tuple-element.10.turn_hbm, ...), custom_call_target="tpu_custom_call" | custom-call | tf_op jit(solution)/shard_map/pallas_call | solution.py:569

commit v5 on v4

--- a/solution.py
+++ b/solution.py
@@ -1,3 +1,5 @@
+import functools
+
 import jax
 import jax.numpy as jnp
 from jax import lax
@@ -69,7 +71,8 @@
     return lax.broadcasted_iota(jnp.int32, shape, dim)
 
 
-def ridge_factor(p):
+def ridge_factor(p, beside=()):
+    beside = list(beside)
     gram = dot6(p, p, NT)
     inv_shift = 1.0 / (jnp.sum(p * p) / N + 1e-06)
     eye = (iota((N, N), 0) == iota((N, N), 1)).astype(F32)
@@ -87,6 +90,8 @@
             e2 = bdot(eh, eh)
             x = w * (x + bdot(x.astype(BF16), eh))
         e = (1.0 - w) * eye + w * e2
+        if beside:
+            beside.pop(0)()
     return b, x, inv_shift
 
 
@@ -413,11 +418,13 @@
     early = swap(0)
     sum_step(0)
     picked = opk[0]
-    factor = ridge_factor(picked)
+    turned = ridge_solve(ridge_factor(picked), picked)
+    turn_out[...] = turned
+    store(turn_out, turn_hbm)
     arrive(stage)
-    ocm[0] = ridge_solve(factor, dot6(picked, mfull[...], NT))
+    ocm[0] = dot6(turned, mfull[...], NT)
     late = offer(ocm, xcm, 0)
-    leaf_factor = factor
+    sum_step(1)
 
     row = iota((AUG, AUG), 0)
     col = iota((AUG, AUG), 1)
@@ -438,20 +445,41 @@
         onehot = onehots[last]
         fresh = bdot(onehot[:, :N], own_f) + bdot(onehot[:, N:], other_f)
         och[level] = dead_rows(fresh, 0, ranks_ref[0, level])
+        ch, cl = split2(coupling)
+        co[:N] = ocm[last]
         arrive(handed[1:])
+        cy[N:] = xpk[last] - dot3(coupling_t, ocm[last])
+        from_other = pick(onehot[:, N:], cy[N:])
         arrive(accept(late, xcm, last))
-        co[:N] = ocm[last]
+        xh, xl = split2(xcm[last])
+        own_new = opk[last] - (bdot(ch, xh) + (bdot(ch, xl) + bdot(cl, xh)))
+        cy[:N] = own_new
+        picked = pick(onehot[:, :N], own_new) + from_other
         co[N:] = xcm[last]
-        cy[:N] = opk[last] - dot3(coupling, xcm[last])
-        cy[N:] = xpk[last] - dot3(coupling_t, ocm[last])
         cand = cy[...]
-        picked = pick(onehot, cand)
         opk[level] = picked
         if level < LEVELS:
             early = swap(level)
-        sum_step(level)
-        factor = ridge_factor(picked)
-        weight = dot6(dot6(picked, cand, NT), co[...])
+        made = {}
+
+        def cross(name, rows):
+            made[name] = dot6(made["p"], cy[rows], NT)
+
+        def apply(name, rows):
+            made[name] = dot6(made[name], co[rows])
+
+        made["p"] = picked
+        own_half, other_half = slice(0, N), slice(N, 2 * N)
+        factor = ridge_factor(
+            picked,
+            [
+                functools.partial(cross, "own", own_half),
+                functools.partial(apply, "own", own_half),
+                functools.partial(cross, "other", other_half),
+                functools.partial(apply, "other", other_half),
+            ],
+        )
+        weight = made["own"] + made["other"]
         if level < LEVELS:
             ocm[level] = ridge_solve(factor, weight)
             late = offer(ocm, xcm, level)
@@ -461,16 +489,13 @@
             top_out[...] = both[:, :N]
             store(top_out, top_hbm.at[0])
             turned = both[:, N:]
-        if level == 1:
-            turn_out[...] = ridge_solve(leaf_factor, opk[0])
-            store(turn_out, turn_hbm)
         interp = dot3(cand, turned, NT)
         at = is_upper[last] * N
         node_out[last, pl.ds(pl.multiple_of(at, N), N), :] = interp[:N]
         node_out[last, pl.ds(pl.multiple_of(N - at, N), N), :] = interp[N:]
         store(node_out.at[last], node_hbm.at[0, last])
-
-    sum_step(4)
+        sum_step(level + 1)
+
     store(tot.at[OWN], diag_hbm)
     for move in stores:
         move.wait()

time: 117 us -> 112 us (0.957)
  Pallas kernels: 116 us -> 111 us
    pallas_call x1, Pallas kernels: 113 us -> 108 us  [shards(): pl.pallas_call(body, out_shape=(jax.ShapeDtypeStruct((N, N), F32), jax.Sh...]
where the time goes in v5:
time: 112 us
  Pallas kernels  111 us (99%)
    pallas_call x1, Pallas kernels, shards(): pl.pallas_call(body, out_shape=(jax.ShapeDtypeStruct((N, N), F32), jax.Sh...  108 us
    pallas_call x1, Pallas kernels, shards(): pl.pallas_call(finish, out_shape=(jax.ShapeDtypeStruct((N, N), F32),) + t...  3.15 us

profile of v5, /device:TPU:1, one launch (start us, length us, event | category | flops | bytes accessed | tf_op | source)
XLA Modules:
  0.0 112.3 jit_solution(12950662550768026046)
XLA Ops:
  0.6 108.3 %shard_map.93 = (f32[256,256]{1,0:T(8,128)}, f32[256,256]{1,0:T(8,128)}, f32[1,3,512,256]{3,2,1,0:T(8,128)}, f32[1,3,256,256]{3,2,1,0:T(8,128)}, f32[1,256,256]{2,1,0:T(8,128)}) custom-call(bf16[256,256]{1,0:T(8,128)(2,1)} %omega_hbm.1, bf16[64,256]{1,0:T(8,128)(2,1)} %bitcast.2, f32[256,256]{1,0:T(8,128)} %samples_hbm.3, s32[1,256]{1,0:T(1,128)} %skel_hbm.1, ...), custom_call_target="tpu_custom_call" | custom-call | tf_op jit(solution)/shard_map/pallas_call | solution.py:537
  108.9 3.1 %shard_map.94 = (f32[256,256]{1,0:T(8,128)}, f32[1,3,512,256]{3,2,1,0:T(8,128)}, f32[1,3,256,256]{3,2,1,0:T(8,128)}, f32[1,256,256]{2,1,0:T(8,128)}) custom-call(f32[256,256]{1,0:T(8,128)} %samples_hbm.3, f32[256,256]{1,0:T(8,128)} %get-tuple-element.9.diag_hbm, f32[256,256]{1,0:T(8,128)} %get-tuple-element.10.turn_hbm, ...), custom_call_target="tpu_custom_call" | custom-call | tf_op jit(solution)/shard_map/pallas_call | solution.py:594

commit v6 on v5

--- a/solution.py
+++ b/solution.py
@@ -80,7 +80,7 @@
     x = ALPHA * eye - BETA * b
     e = eye - dot3(b, x)
     for step, w in enumerate(RATES):
-        if step < 4:
+        if step < 3:
             eh, el = split2(e)
             xh, xl = split2(x)
             e2 = bdot(eh, eh) + (bdot(eh, el) + bdot(el, eh))
@@ -399,18 +399,23 @@
 
     core = leaf % 2
     mate = partners[0]
-    mine = pl.ds(pl.multiple_of(core * hr, hr), hr)
+    quarter = N // 4
+    mine = [pl.ds(pl.multiple_of(core * hr + i * quarter, quarter), quarter) for i in range(2)]
 
     def offer(src, dst, level):
         if level == 0:
             return [send(src.at[0], dst.at[0], mate)]
-        return [send(src.at[level, mine], dst.at[level, mine], partners[level])]
+        return [send(src.at[level, at], dst.at[level, at], partners[level]) for at in mine]
 
     def accept(group, dst, level):
-        arrive(group)
-        if level > 0:
-            return [send(dst.at[level, mine], dst.at[level, mine], mate)]
-        return []
+        if level == 0:
+            arrive(group)
+            return []
+        handed = []
+        for copy, at in zip(group, mine):
+            copy.wait_recv()
+            handed.append(send(dst.at[level, at], dst.at[level, at], mate))
+        return handed
 
     def swap(level):
         return [offer(och, xch, level), offer(opk, xpk, level)]
@@ -433,8 +438,9 @@
 
     for level in range(1, LEVELS + 1):
         last = level - 1
-        handed = accept(early[0], xch, last) + accept(early[1], xpk, last)
-        arrive(handed[:1])
+        handed = accept(early[0], xch, last)
+        handed_rows = accept(early[1], xpk, last)
+        arrive(handed)
         own_f, other_f = och[last], xch[last]
         own_g = bdot(own_f, turn).astype(BF16)
         other_g = bdot(other_f, turn).astype(BF16)
@@ -447,7 +453,7 @@
         och[level] = dead_rows(fresh, 0, ranks_ref[0, level])
         ch, cl = split2(coupling)
         co[:N] = ocm[last]
-        arrive(handed[1:])
+        arrive(handed_rows)
         cy[N:] = xpk[last] - dot3(coupling_t, ocm[last])
         from_other = pick(onehot[:, N:], cy[N:])
         arrive(accept(late, xcm, last))
@@ -530,7 +536,7 @@
         store.wait()
 
 
-N_COPIES = 14 * PIECES + 6 * (RING - 1) + 6 * (RING - 1) + 8 + 3 + 6 * (LEVELS - 1)
+N_COPIES = 14 * PIECES + 6 * (RING - 1) + 6 * (RING - 1) + 8 + 3 + 12 * (LEVELS - 1)
 
 
 def shards(points, omega, samples, ranks, leaf_skeleton, merge_skeleton):

time: 112 us -> 112 us (level)
  no operation moved by 1% of the time
where the time goes in v6:
time: 112 us
  Pallas kernels  111 us (99%)
    pallas_call x1, Pallas kernels, shards(): pl.pallas_call(body, out_shape=(jax.ShapeDtypeStruct((N, N), F32), jax.Sh...  108 us
    pallas_call x1, Pallas kernels, shards(): pl.pallas_call(finish, out_shape=(jax.ShapeDtypeStruct((N, N), F32),) + t...  3.15 us

profile of v6, /device:TPU:1, one launch (start us, length us, event | category | flops | bytes accessed | tf_op | source)
XLA Modules:
  0.0 112.2 jit_solution(6649107540863043729)
XLA Ops:
  0.6 108.2 %shard_map.93 = (f32[256,256]{1,0:T(8,128)}, f32[256,256]{1,0:T(8,128)}, f32[1,3,512,256]{3,2,1,0:T(8,128)}, f32[1,3,256,256]{3,2,1,0:T(8,128)}, f32[1,256,256]{2,1,0:T(8,128)}) custom-call(bf16[256,256]{1,0:T(8,128)(2,1)} %omega_hbm.1, bf16[64,256]{1,0:T(8,128)(2,1)} %bitcast.2, f32[256,256]{1,0:T(8,128)} %samples_hbm.3, s32[1,256]{1,0:T(1,128)} %skel_hbm.1, ...), custom_call_target="tpu_custom_call" | custom-call | tf_op jit(solution)/shard_map/pallas_call | solution.py:543
  108.8 3.1 %shard_map.94 = (f32[256,256]{1,0:T(8,128)}, f32[1,3,512,256]{3,2,1,0:T(8,128)}, f32[1,3,256,256]{3,2,1,0:T(8,128)}, f32[1,256,256]{2,1,0:T(8,128)}) custom-call(f32[256,256]{1,0:T(8,128)} %samples_hbm.3, f32[256,256]{1,0:T(8,128)} %get-tuple-element.9.diag_hbm, f32[256,256]{1,0:T(8,128)} %get-tuple-element.10.turn_hbm, ...), custom_call_target="tpu_custom_call" | custom-call | tf_op jit(solution)/shard_map/pallas_call | solution.py:600
